TPU v7x, 128 devices: a whole 4x4x4 slice. The times are simulated.
128 devices in a mesh: tm: 4 (over y), rest: 32 (over x, z, core).
Axes of the slice: x: 4, y: 4, z: 4, core: 2. Of those that a mesh axis runs over, the one named last changes fastest.
Arguments:
- slab: float32 [1024, 131072], P('tm', 'rest')
- start_basis: float32 [1024, 128], replicated, may hold values from -6 to 6
- time_rank: int32 [1], replicated, may hold values from 64 to 128
Outputs:
- basis: float32 [1024, 128], replicated
- core: float32 [128, 131072], P('tm', 'rest')
- param_gram: float32 [128, 128], replicated
All inputs are finite; a program needn't handle non-finite values.
Results may differ from a plain program's by a relative error of at most 0.0003.
Values sent between devices are 32-bit elements; how exact they have to be, the bound alone decides.
No kernel may reach another device: no remote copies, remote signals or barrier semaphores. Data moves between devices by JAX's collectives and lax.ppermute only.
A program may use at most 128 MiB of HBM per device.

v0:
```python
import jax
import jax.numpy as jnp
from jax import lax
from jax.experimental import pallas as pl
from jax.experimental.pallas import tpu as pltpu
from jax.sharding import PartitionSpec as P

F32, BF16 = jnp.float32, jnp.bfloat16
PARAMS = 128
ITERS = 3
HELD = 56
COST = {"own_gram": 10**9, "early_gram": 10**9, "late_gram": 2 * 10**10}
NY, NX, NZ = 4, 4, 4
VMEM, SMEM, HBM = pltpu.VMEM, pltpu.SMEM, pltpu.HBM


def rest_index(x, z, c):
    return (x * NZ + z) * 2 + c


def along_y(v, k):
    return lax.ppermute(v, "tm", [(i, (i + k) % NY) for i in range(NY)])


def along_core(v):
    return lax.ppermute(v, "rest", [(i, i ^ 1) for i in range(2 * NX * NZ)])


def along_xz(v, k, first):
    perm = []
    for x in range(NX):
        for z in range(NZ):
            for c in range(2):
                if (c == 0) == first:
                    to = rest_index((x + k) % NX, z, c)
                else:
                    to = rest_index(x, (z + k) % NZ, c)
                perm.append((rest_index(x, z, c), to))
    return lax.ppermute(v, "rest", perm)


def position():
    me_y, rest = lax.axis_index("tm"), lax.axis_index("rest")
    core, z, x = lax.rem(rest, 2), lax.rem(lax.div(rest, 2), NZ), lax.div(rest, 2 * NZ)
    return me_y, core, jnp.where(core == 0, x, z), jnp.where(core == 0, z, x)


def around(i, k):
    return lax.rem(i + k, 4)


def low_first(me, i, j):
    swap = around(me, i) > around(me, j)
    return jnp.where(swap, j, i), jnp.where(swap, i, j)


def split2(v):
    hi = v.astype(BF16)
    return hi, (v - hi.astype(F32)).astype(BF16)


def split3(v):
    hi = v.astype(BF16)
    rest = v - hi.astype(F32)
    mid = rest.astype(BF16)
    return hi, mid, (rest - mid.astype(F32)).astype(BF16)


def dot(a, b, ca, cb):
    return lax.dot_general(a, b, (((ca,), (cb,)), ((), ())), preferred_element_type=F32)


def product(hl, i, j, core, out):
    h, l = hl.at[i], hl.at[j]
    total = dot(h[0], l[0], 1, 1) + (dot(h[1], l[0], 1, 1) + dot(h[0], l[1], 1, 1) + dot(h[1], l[1], 1, 1))
    half = total.shape[0] // 2
    out[0][...] = jnp.where(core == 0, total[half:], total[:half])
    out[1][...] = jnp.where(core == 0, total[:half], total[half:])


def own_kernel(slab, send, keep, hl_out, across, hl, sem):
    me_y, core, _, _ = position()
    h, l = split2(slab[...])
    hl[0, 0], hl[0, 1] = h, l
    width = hl_out.shape[2]
    mine = pl.ds(pl.multiple_of(me_y * width, 128), width)
    theirs = pl.ds(pl.multiple_of(around(me_y, 2) * width, 128), width)
    outs = [
        pltpu.make_async_copy(hl.at[0, :, :, mine], hl_out, sem.at[0]),
        pltpu.make_async_copy(slab.at[:, theirs], across, sem.at[1]),
    ]
    for out in outs:
        out.start()
    product(hl, 0, 0, core, (send, keep))
    for out in outs:
        out.wait()


def slices_kernel(slab, ahead, behind, sem):
    me_y = lax.axis_index("tm")
    width = ahead.shape[1]
    outs = []
    for n, (k, out) in enumerate(((1, ahead), (3, behind))):
        at = pl.ds(pl.multiple_of(around(me_y, k) * width, 128), width)
        outs.append(pltpu.make_async_copy(slab.at[:, at], out, sem.at[n]))
    for out in outs:
        out.start()
    for out in outs:
        out.wait()


def slices(slab):
    out = jax.ShapeDtypeStruct((slab.shape[0], slab.shape[1] // NY), F32)
    hbm = pl.BlockSpec(memory_space=HBM)
    return pl.pallas_call(
        slices_kernel,
        out_shape=[out, out],
        in_specs=[hbm],
        out_specs=[pl.BlockSpec(memory_space=VMEM)] * 2,
        scratch_shapes=[pltpu.SemaphoreType.DMA((2,))],
        compiler_params=pltpu.CompilerParams(vmem_limit_bytes=56 * 2**20),
        name="slices",
    )(slab)


def early_kernel(w1, w3, send0, keep0, hl0, send, keep, hls, hl, sem):
    me_y, core, _, _ = position()
    copy = pltpu.make_async_copy(hl0, hl.at[0], sem.at[0])
    copy.start()
    for w, d in ((w1, 3), (w3, 1)):
        h, l = split2(w[...])
        hl[d, 0], hl[d, 1] = h, l
    outs = [pltpu.make_async_copy(hl.at[d], hls.at[d], sem.at[d]) for d in (1, 3, 0)]
    for out in outs[:2]:
        out.start()
    send[0], keep[0] = send0[...], keep0[...]
    copy.wait()
    outs[2].start()
    for n, (i, j) in enumerate(((0, 1), (3, 0), low_first(me_y, 3, 1))):
        product(hl, i, j, core, (send.at[n + 1], keep.at[n + 1]))
    for out in outs:
        out.wait()


def late_kernel(w2, hls, send, keep, hl, sem):
    me_y, core, _, _ = position()
    copies = [pltpu.make_async_copy(hls.at[d], hl.at[d], sem.at[d]) for d in (0, 3, 1)]
    for copy in copies:
        copy.start()
    h, l = split2(w2[...])
    hl[2, 0], hl[2, 1] = h, l
    for n, (i, j) in enumerate((low_first(me_y, 0, 2), (2, 3), (1, 2))):
        copies[n].wait()
        product(hl, i, j, core, (send.at[n], keep.at[n]))


def gram_call(kernel, name, vmem_args, hbm_args, blocks, wide, halves, cols):
    rows = 256
    struct = jax.ShapeDtypeStruct
    vmem, hbm = pl.BlockSpec(memory_space=VMEM), pl.BlockSpec(memory_space=HBM)
    half = struct((blocks, rows // 2, rows) if blocks else (rows // 2, rows), F32)
    slots = NY if hbm_args else 1
    return pl.pallas_call(
        kernel,
        out_shape=[half, half] + [struct((2, rows, cols) if blocks == 0 else (HELD, 2, rows, cols), BF16)] * halves + [struct((rows, cols), F32)] * (1 - slots // NY),
        in_specs=[vmem] * len(vmem_args) + [hbm] * len(hbm_args),
        out_specs=[vmem] * 2 + [hbm] * (halves + 1 - slots // NY),
        scratch_shapes=[VMEM((slots, 2, rows, wide), BF16), pltpu.SemaphoreType.DMA((NY,))],
        compiler_params=pltpu.CompilerParams(vmem_limit_bytes=16 * 2**20),
        cost_estimate=pl.CostEstimate(flops=COST.get(name, 10**9), bytes_accessed=1000, transcendentals=0),
        name=name,
    )(*vmem_args, *hbm_args)


def row_of(v, k):
    return jnp.broadcast_to(v[k : k + 1, :], v.shape)


def cholesky_inverse(work):
    n = work.shape[0]
    panels = n // 8
    r = lax.broadcasted_iota(jnp.int32, (n, n), 0)
    c = lax.broadcasted_iota(jnp.int32, (n, n), 1)
    work[:, n:] = (r == c).astype(F32)
    row = lax.broadcasted_iota(jnp.int32, (8, n), 0)
    left, right = {}, {}

    def load(t):
        left[t], right[t] = work[8 * t : 8 * t + 8, :n], work[8 * t : 8 * t + 8, n:]

    def columns(t, p):
        return [jnp.broadcast_to(left[t][:, 8 * p + j : 8 * p + j + 1], (8, n)) for j in range(8)]

    for t in range(2):
        load(t)
    column = columns(0, 0)
    for p in range(panels):
        first = p - p % 2
        if p == first:
            for t in range(first + 2, min(first + 4, panels)):
                load(t)
        below = range(p + 1, min(first + 4, panels))
        entries = {t: columns(t, p) for t in below}
        ahead = columns(p + 1, p + 1) if below else None
        scale = jnp.zeros((8, n), F32)
        for k in range(8):
            pivot = row_of(column[k], k)
            inverse = 1.0 / pivot
            scale = jnp.where(row == k, lax.rsqrt(pivot), scale)
            factor = jnp.where(row > k, column[k] * inverse, 0.0)
            across = [row_of(column[j], k) for j in range(k + 1, 8)]
            for j in range(k + 1, 8):
                column[j] = column[j] - factor * across[j - k - 1]
            left_k, right_k = row_of(left[p], k), row_of(right[p], k)
            left[p], right[p] = left[p] - factor * left_k, right[p] - factor * right_k
            for t in below:
                factor = entries[t][k] * inverse
                if t == p + 1:
                    ahead = [ahead[j] - factor * row_of(entries[t][k], j) for j in range(8)]
                for j in range(k + 1, 8):
                    entries[t][j] = entries[t][j] - factor * across[j - k - 1]
                left[t], right[t] = left[t] - factor * left_k, right[t] - factor * right_k
        left[p], right[p] = left[p] * scale, right[p] * scale
        if p > first and first + 4 < panels:
            h, m, l = split3(jnp.concatenate([jnp.concatenate([left[t], right[t]], 1) for t in (first, p)], 0))
            lh, lm, ll = h[:, :n], m[:, :n], l[:, :n]
            update = dot(jnp.concatenate([lh, lh, lm, lm, lh, ll], 0), jnp.concatenate([h, m, h, m, l, h], 0), 0, 0)
            start = 8 * (first + 4)
            work[start:, :] = work[start:, :] - update[start:]
        column = ahead
    return jnp.concatenate([right[p] for p in range(panels)], 0)


def solve_kernel(rank, *refs, scale):
    me_y, core_id, first, second = position()
    pieces, start, hls, w2 = refs[:8], refs[8], refs[9], refs[10]
    basis_out, core0, core1, core2, core3, param_out = refs[11:17]
    packed, gh, gm, gl, hl, last, work, core, qhl, iterate, sem = refs[17:]
    ends = [(w2, last) if d == 2 else (hls.at[d], hl.at[d]) for d in range(NY)]
    copies = [pltpu.make_async_copy(x, y, sem.at[d]) for d, (x, y) in enumerate(ends)]
    for copy in copies:
        copy.start()
    blocks, rows, t = pieces[0].shape
    for n, piece in enumerate(pieces):
        half, base = (core_id, first) if n < NX else (1 - core_id, second)
        at = pl.multiple_of(half * (t // 2) + around(base, NX - n % NX) * rows, rows)
        packed[:, pl.ds(at, rows), :] = piece[...]
    for n, (i, j) in enumerate(
        [(around(me_y, d), around(me_y, d + 1)) for d in range(NY)]
        + [tuple(around(me_y, d) for d in low_first(me_y, e, e + 2)) for e in range(2)]
        + [(around(me_y, d), around(me_y, d)) for d in range(NY)]
    ):
        block = packed[n] * scale
        for k, g in enumerate(split3(block)):
            (gh, gm, gl)[k][i, :, pl.ds(pl.multiple_of(j * t, t), t)] = g
        if n < 6:
            for k, g in enumerate(split3(block.T)):
                (gh, gm, gl)[k][j, :, pl.ds(pl.multiple_of(i * t, t), t)] = g

    iterate[...] = start[...].T
    n = iterate.shape[0]

    def step(_, carry):
        h, m, l = split3(iterate[...])
        by_h = dot(jnp.concatenate([h, m, l], 0), gh[...].reshape(NY * t, NY * t), 1, 0)
        by_m = dot(jnp.concatenate([h, m], 0), gm[...].reshape(NY * t, NY * t), 1, 0)
        by_l = dot(h, gl[...].reshape(NY * t, NY * t), 1, 0)
        image = by_h[:n] + ((by_h[n : 2 * n] + by_m[:n]) + (by_h[2 * n :] + by_m[n:] + by_l))
        h, m, l = split3(image)
        by_h = dot(jnp.concatenate([h, m, l], 0), h, 1, 1)
        small = by_h[n : 2 * n] + by_h[2 * n :]
        work[:, :n] = by_h[:n] + ((small + small.T) + dot(m, m, 1, 1))
        ih, im, il = split3(cholesky_inverse(work))
        by_h = dot(jnp.concatenate([ih, im, il], 0), h, 1, 0)
        by_m = dot(jnp.concatenate([ih, im], 0), m, 1, 0)
        iterate[...] = by_h[:n] + ((by_h[n : 2 * n] + by_m[:n]) + (by_h[2 * n :] + by_m[n:] + dot(ih, l, 1, 0)))
        return carry

    lax.fori_loop(0, ITERS, step, 0)
    q = iterate[...]
    slot = lax.broadcasted_iota(jnp.int32, q.shape, 0)
    q = jnp.where(slot < rank[0], q, 0.0)
    basis_out[...] = q.T
    qhl[0], qhl[1] = split2(q)
    total = None
    for d in range(NY):
        copies[d].wait()
        if d == 2:
            hl[2, 0], hl[2, 1] = split2(last[...])
        at = pl.ds(pl.multiple_of(around(me_y, d) * t, t), t)
        hs, ls = qhl[0, :, at], qhl[1, :, at]
        by_hi = dot(jnp.concatenate([hs, ls], 0), hl[d, 0], 1, 0)
        term = by_hi[:n] + (by_hi[n:] + dot(hs, hl[d, 1], 1, 0))
        total = term if total is None else total + term
    core[...] = total
    own = n // NY
    for k, out in enumerate((core0, core1, core2, core3)):
        out[...] = core[pl.ds(pl.multiple_of(around(me_y, k) * own, 8), own), :]
    h, l = split2(total)
    param = jnp.zeros((PARAMS, PARAMS), F32)
    for s in range(total.shape[1] // PARAMS):
        hs, ls = h[:, s * PARAMS : (s + 1) * PARAMS], l[:, s * PARAMS : (s + 1) * PARAMS]
        cross = dot(hs, ls, 0, 0)
        param = param + (dot(hs, hs, 0, 0) + (cross + cross.T) + dot(ls, ls, 0, 0))
    param_out[...] = param


def solve(rank, pieces, start_basis, hls, w2, scale):
    time_all, ranks = start_basis.shape
    blocks, _, t = pieces[0].shape
    width = w2.shape[1]
    struct = jax.ShapeDtypeStruct
    part = struct((ranks // NY, width), F32)
    vmem = pl.BlockSpec(memory_space=VMEM)
    smem = pl.BlockSpec(memory_space=SMEM)
    hbm = pl.BlockSpec(memory_space=HBM)

    def body(*refs):
        solve_kernel(*refs, scale=scale)

    return pl.pallas_call(
        body,
        out_shape=(struct((time_all, ranks), F32), part, part, part, part, struct((PARAMS, PARAMS), F32)),
        in_specs=[smem] + [vmem] * 9 + [hbm] * 2,
        out_specs=[vmem] * 6,
        scratch_shapes=[
            VMEM((blocks, t, t), F32),
            VMEM((NY, t, time_all), BF16),
            VMEM((NY, t, time_all), BF16),
            VMEM((NY, t, time_all), BF16),
            VMEM((NY, 2, t, width), BF16),
            VMEM((t, width), F32),
            VMEM((ranks, 2 * ranks), F32),
            VMEM((ranks, width), F32),
            VMEM((2, ranks, time_all), BF16),
            VMEM((ranks, time_all), F32),
            pltpu.SemaphoreType.DMA((NY,)),
        ],
        compiler_params=pltpu.CompilerParams(vmem_limit_bytes=28 * 2**20),
        cost_estimate=pl.CostEstimate(flops=8 * 10**9, bytes_accessed=9 * 2**20, transcendentals=0),
        name="solve",
    )(rank, *pieces, start_basis, hls, w2)


def join_kernel(p0, p1, p2, p3, out):
    me_y = lax.axis_index("tm")
    width = p0.shape[1]
    for k, piece in enumerate((p0, p1, p2, p3)):
        out[:, pl.ds(pl.multiple_of(around(me_y, NY - k) * width, 128), width)] = piece[...]


def join_columns(pieces):
    rows, width = pieces[0].shape
    return pl.pallas_call(
        join_kernel,
        out_shape=jax.ShapeDtypeStruct((rows, NY * width), F32),
        in_specs=[pl.BlockSpec(memory_space=VMEM)] * 4,
        out_specs=pl.BlockSpec(memory_space=VMEM),
        compiler_params=pltpu.CompilerParams(vmem_limit_bytes=4 * 2**20),
        name="join_columns",
    )(*pieces)


def scatter_sum(v, me, move):
    v = v.reshape(v.shape[0], NX, v.shape[1] // NX, v.shape[2])

    def slot(k):
        return lax.dynamic_index_in_dim(v, (me + k) % NX, 1, keepdims=False)

    got = [move(slot(k), k) for k in (1, 3, 2)]
    return slot(0) + got[0] + got[1] + got[2]


def exchange_sum(v, move):
    got = [move(v, k) for k in (1, 3, 2)]
    return v + got[0] + got[1] + got[2]


def gather(v, move):
    got = {k: move(v, k) for k in (1, 3, 2)}
    return [v, got[1], got[2], got[3]]


def local(slab, start_basis, time_rank):
    rest_count = lax.axis_size("rest")
    columns_local = slab.shape[1]
    columns_all = columns_local * rest_count
    width = columns_local // NY
    ranks = start_basis.shape[1]
    _, _, first_me, _ = position()

    def scatter(send, keep):
        return scatter_sum(keep + along_core(send), first_me, lambda w, k: along_xz(w, k, True))

    def exchange(u):
        return exchange_sum(u, lambda w, k: along_xz(w, k, False))

    next_cols, last_cols = slices(slab)
    w1, w3 = along_y(next_cols, 1), along_y(last_cols, 3)
    send0, keep0, hl0, across = gram_call(own_kernel, "own_gram", [slab], [], 0, columns_local, 1, width)
    w1, w3, across = lax.optimization_barrier((w1, w3, across))
    w2 = along_y(across, 2)
    send, keep, hls = gram_call(early_kernel, "early_gram", [w1, w3, send0, keep0], [hl0], 4, width, 1, width)
    early = scatter(send, keep)
    early, w2 = lax.optimization_barrier((early, w2))
    early = exchange(early)
    send, keep = gram_call(late_kernel, "late_gram", [w2], [hls], 3, width, 0, width)
    late = exchange(scatter(send, keep))
    v = jnp.concatenate([early, late])
    got = {k: along_y(v, k) for k in (1, 3, 2)}
    at = [v, got[3], got[2], got[1]]

    def term(d, n):
        return at[d % NY][n]

    v = jnp.stack(
        [term(d, 1) + term(d + 1, 2) + term(d + 2, 5) + term(d + 3, 6) for d in range(NY)]
        + [term(d, 4) + term(d + 2, 4) + term(d + 1, 3) + term(d + 3, 3) for d in range(2)]
        + [term(d, 0) for d in range(NY)]
    )
    pieces = gather(v, lambda u, k: along_xz(u, k, True))
    pieces = pieces + [along_core(piece) for piece in pieces]
    basis, *cores, param = solve(time_rank, pieces, start_basis, hls, w2, 1.0 / columns_all)

    param = param + along_core(param)
    param = exchange_sum(param, lambda u, k: along_xz(u, k, True))
    param = exchange_sum(param, lambda u, k: along_xz(u, k, False))
    param = exchange_sum(param, along_y)
    space_all = columns_local // PARAMS * rest_count
    param_gram = param / float(ranks * space_all)

    mine = {k: along_y(cores[k], k) for k in (1, 3, 2)}
    core = join_columns([cores[0], mine[1], mine[2], mine[3]])
    return (basis, core, param_gram)


def solution(mesh):
    in_specs = (P("tm", "rest"), P(), P())
    out_specs = (P(), P("tm", "rest"), P())
    return jax.shard_map(local, mesh=mesh, in_specs=in_specs, out_specs=out_specs, check_vma=False)
```

profile of v0, /device:TPU:0, one launch (start us, length us, event | category | flops | bytes accessed | tf_op | source)
XLA Modules:
  0.0 160.6 jit_solution(3453109422527608075)
XLA Ops:
  0.6 3.0 %slices.1 = (f32[256,1024]{1,0:T(8,128)}, f32[256,1024]{1,0:T(8,128)}) custom-call(f32[256,4096]{1,0:T(8,128)} %slab.3), custom_call_target="tpu_custom_call" | custom-call | tf_op jit(solution)/shard_map/slices/pallas_call | solution.py:115
  3.6 1.7 %collective-permute-start = (f32[256,1024]{1,0:T(8,128)}, f32[256,1024]{1,0:T(8,128)S(1)}, u32[]{:S(2)}, u32[]{:S(2)}) collective-permute-start(f32[256,1024]{1,0:T(8,128)} %get-tuple-element.25), channel_id=1, source_target_pairs={{0,32},{32,64},{64,96},{96,0},{1,33},{33,65},{65,97},{97,1},{2,34}... | collective-permute-start | bytes 3145736 | tf_op jit(solution)/shard_map/ppermute | solution.py:22
  5.3 1.6 collective-permute-start.1
  6.9 2.2 %copy-done = f32[256,4096]{1,0:T(8,128)S(1)} copy-done((f32[256,4096]{1,0:T(8,128)S(1)}, f32[256,4096]{1,0:T(8,128)}, u32[]{:S(2)}) %copy-start) | copy-done | bytes 4194328
  9.1 3.4 %own_gram.1 = (f32[128,256]{1,0:T(8,128)S(1)}, f32[128,256]{1,0:T(8,128)S(1)}, bf16[2,256,1024]{2,1,0:T(8,128)(2,1)S(1)}, f32[256,1024]{1,0:T(8,128)S(1)}) custom-call(f32[256,4096]{1,0:T(8,128)S(1)} %copy-done), custom_call_target="tpu_custom_call" | custom-call | flops 1000000000 | bytes 1000 | tf_op jit(solution)/shard_map/own_gram/pallas_call | solution.py:163
  12.5 17.7 %collective-permute-done.w1 = f32[256,1024]{1,0:T(8,128)S(1)} collective-permute-done((f32[256,1024]{1,0:T(8,128)}, f32[256,1024]{1,0:T(8,128)S(1)}, u32[]{:S(2)}, u32[]{:S(2)}) %collective-permute-start) | collective-permute-done | bytes 1048608 | tf_op jit(solution)/shard_map/ppermute | solution.py:22
  30.2 2.9 %collective-permute-start.6 = (f32[256,1024]{1,0:T(8,128)S(1)}, f32[256,1024]{1,0:T(8,128)S(1)}, u32[]{:S(2)}, u32[]{:S(2)}) collective-permute-start(f32[256,1024]{1,0:T(8,128)S(1)} %get-tuple-element.35), channel_id=1, source_target_pairs={{0,64},{32,96},{64,0},{96,32},{1,65},{33,97},{65,1},{97,33},{2,66}... | collective-permute-start | bytes 3145736 | tf_op jit(solution)/shard_map/ppermute | solution.py:22
  33.1 3.3 %early_gram.1 = (f32[4,128,256]{2,1,0:T(8,128)}, f32[4,128,256]{2,1,0:T(8,128)S(1)}, bf16[56,2,256,1024]{3,2,1,0:T(8,128)(2,1)}) custom-call(f32[256,1024]{1,0:T(8,128)S(1)} %collective-permute-done.w1, f32[256,1024]{1,0:T(8,128)S(1)} %collective-permute-done.1.w3, f32[128,256]{1,0:T(8,128)S(1)} %get-tuple-element.30.send0, ...), custom_call_target="tpu_custom_call" | custom-call | flops 1000000000 | bytes 1000 | tf_op jit(solution)/shard_map/early_gram/pallas_call | solution.py:163
  36.6 2.2 %collective-permute-done.2 = f32[4,128,256]{2,1,0:T(8,128)} collective-permute-done((f32[4,128,256]{2,1,0:T(8,128)}, f32[4,128,256]{2,1,0:T(8,128)}, u32[]{:S(2)}, u32[]{:S(2)}) %collective-permute-start.2) | collective-permute-done | bytes 524320 | tf_op jit(solution)/shard_map/ppermute | solution.py:26
  38.8 1.1 add.191
  39.9 0.8 copy-done.2
  40.7 3.1 %collective-permute-start.5 = (f32[4,32,256]{2,1,0:T(8,128)S(1)}, f32[4,32,256]{2,1,0:T(8,128)S(1)}, u32[]{:S(2)}, u32[]{:S(2)}) collective-permute-start(f32[4,32,256]{2,1,0:T(8,128)S(1)} %get-tuple-element.49), channel_id=1, source_target_pairs={{0,16},{1,5},{2,18},{3,7},{4,20},{5,1},{6,22},{7,3},{8,24},{9,13},... | collective-permute-start | bytes 393224 | tf_op jit(solution)/shard_map/ppermute | solution.py:39
  43.8 1.1 collective-permute-start.4
  44.9 0.9 collective-permute-start.3
  45.8 1.4 collective-permute-done.5
  47.2 1.5 collective-permute-done.4
  48.8 2.4 %collective-permute-done.3 = f32[4,32,256]{2,1,0:T(8,128)S(1)} collective-permute-done((f32[4,32,256]{2,1,0:T(8,128)S(1)}, f32[4,32,256]{2,1,0:T(8,128)S(1)}, u32[]{:S(2)}, u32[]{:S(2)}) %collective-permute-start.3) | collective-permute-done | bytes 131104 | tf_op jit(solution)/shard_map/ppermute | solution.py:39
  51.1 0.9 fusion.1
  52.1 3.8 %collective-permute-done.6.w2.refs_11_ = f32[256,1024]{1,0:T(8,128)S(1)} collective-permute-done((f32[256,1024]{1,0:T(8,128)S(1)}, f32[256,1024]{1,0:T(8,128)S(1)}, u32[]{:S(2)}, u32[]{:S(2)}) %collective-permute-start.6) | collective-permute-done | bytes 1048608 | tf_op jit(solution)/shard_map/ppermute | solution.py:22
  55.8 4.5 %late_gram.1 = (f32[3,128,256]{2,1,0:T(8,128)S(1)}, f32[3,128,256]{2,1,0:T(8,128)S(1)}) custom-call(f32[256,1024]{1,0:T(8,128)S(1)} %collective-permute-done.6.w2.refs_11_, bf16[56,2,256,1024]{3,2,1,0:T(8,128)(2,1)} %get-tuple-element.38.hls.refs_10_), custom_call_target="tpu_custom_call" | custom-call | flops 20000000000 | bytes 1000 | tf_op jit(solution)/shard_map/late_gram/pallas_call | solution.py:163
  60.5 1.7 %collective-permute-done.10 = f32[3,128,256]{2,1,0:T(8,128)S(1)} collective-permute-done((f32[3,128,256]{2,1,0:T(8,128)S(1)}, f32[3,128,256]{2,1,0:T(8,128)S(1)}, u32[]{:S(2)}, u32[]{:S(2)}) %collective-permute-start.10) | collective-permute-done | bytes 393248 | tf_op jit(solution)/shard_map/ppermute | solution.py:26
  62.3 3.0 %collective-permute-start.13 = (f32[3,32,256]{2,1,0:T(8,128)S(1)}, f32[3,32,256]{2,1,0:T(8,128)S(1)}, u32[]{:S(2)}, u32[]{:S(2)}) collective-permute-start(f32[3,32,256]{2,1,0:T(8,128)S(1)} %get-tuple-element.52), channel_id=1, source_target_pairs={{0,16},{1,5},{2,18},{3,7},{4,20},{5,1},{6,22},{7,3},{8,24},{9,13},... | collective-permute-start | bytes 294920 | tf_op jit(solution)/shard_map/ppermute | solution.py:39
  65.3 1.1 collective-permute-start.12
  66.4 0.9 collective-permute-start.11
  67.3 3.9 %collective-permute-start.9 = (f32[4,32,256]{2,1,0:T(8,128)S(1)}, f32[4,32,256]{2,1,0:T(8,128)S(1)}, u32[]{:S(2)}, u32[]{:S(2)}) collective-permute-start(f32[4,32,256]{2,1,0:T(8,128)S(1)} %fusion.1), channel_id=1, source_target_pairs={{0,4},{1,17},{2,6},{3,19},{4,0},{5,21},{6,2},{7,23},{8,12},{9,25},... | collective-permute-start | bytes 393224 | tf_op jit(solution)/shard_map/ppermute | solution.py:39
  71.2 0.7 collective-permute-start.8
  71.9 1.3 collective-permute-start.7
  73.2 0.4 collective-permute-done.11
  73.7 2.7 %collective-permute-start.16 = (f32[3,32,256]{2,1,0:T(8,128)S(1)}, f32[3,32,256]{2,1,0:T(8,128)S(1)}, u32[]{:S(2)}, u32[]{:S(2)}) collective-permute-start(f32[3,32,256]{2,1,0:T(8,128)S(1)} %fusion.3), channel_id=1, source_target_pairs={{0,4},{1,17},{2,6},{3,19},{4,0},{5,21},{6,2},{7,23},{8,12},{9,25},... | collective-permute-start | bytes 294920 | tf_op jit(solution)/shard_map/ppermute | solution.py:39
  76.4 1.4 collective-permute-start.15
  77.8 0.6 collective-permute-start.14
  78.5 1.4 collective-permute-done.16
  79.9 1.5 collective-permute-done.15
  81.4 2.2 %collective-permute-done.14 = f32[3,32,256]{2,1,0:T(8,128)S(1)} collective-permute-done((f32[3,32,256]{2,1,0:T(8,128)S(1)}, f32[3,32,256]{2,1,0:T(8,128)S(1)}, u32[]{:S(2)}, u32[]{:S(2)}) %collective-permute-start.14) | collective-permute-done | bytes 98336 | tf_op jit(solution)/shard_map/ppermute | solution.py:39
  83.7 1.3 collective-permute-start.19
  85.0 3.1 %collective-permute-start.18 = (f32[7,32,256]{2,1,0:T(8,128)S(1)}, f32[7,32,256]{2,1,0:T(8,128)S(1)}, u32[]{:S(2)}, u32[]{:S(2)}) collective-permute-start(f32[7,32,256]{2,1,0:T(8,128)S(1)} %pad_maximum_fusion), channel_id=1, source_target_pairs={{0,64},{32,96},{64,0},{96,32},{1,65},{33,97},{65,1},{97,33},{2,66}... | collective-permute-start | bytes 688136 | tf_op jit(solution)/shard_map/ppermute | solution.py:22
  88.0 0.9 collective-permute-start.17
  88.9 3.5 %collective-permute-done.19 = f32[7,32,256]{2,1,0:T(8,128)S(1)} collective-permute-done((f32[7,32,256]{2,1,0:T(8,128)S(1)}, f32[7,32,256]{2,1,0:T(8,128)S(1)}, u32[]{:S(2)}, u32[]{:S(2)}) %collective-permute-start.19) | collective-permute-done | bytes 229408 | tf_op jit(solution)/shard_map/ppermute | solution.py:22
  92.4 2.5 %collective-permute-done.18 = f32[7,32,256]{2,1,0:T(8,128)S(1)} collective-permute-done((f32[7,32,256]{2,1,0:T(8,128)S(1)}, f32[7,32,256]{2,1,0:T(8,128)S(1)}, u32[]{:S(2)}, u32[]{:S(2)}) %collective-permute-start.18) | collective-permute-done | bytes 229408 | tf_op jit(solution)/shard_map/ppermute | solution.py:22
  95.0 0.9 collective-permute-start.20
  95.9 1.8 %collective-permute-start.21 = (f32[10,32,256]{2,1,0:T(8,128)S(1)}, f32[10,32,256]{2,1,0:T(8,128)S(1)}, u32[]{:S(2)}, u32[]{:S(2)}) collective-permute-start(f32[10,32,256]{2,1,0:T(8,128)S(1)} %slice_dynamic-update-slice_fusion.refs_1_), channel_id=1, source_target_pairs={{0,16},{1,5},{2,18},{3,7},{4,20},{5,1},{6,22},{7,3},{8,24},{9,13},... | collective-permute-start | bytes 983048 | tf_op jit(solution)/shard_map/ppermute | solution.py:39
  97.7 1.9 %collective-permute-start.22 = (f32[10,32,256]{2,1,0:T(8,128)S(1)}, f32[10,32,256]{2,1,0:T(8,128)S(1)}, u32[]{:S(2)}, u32[]{:S(2)}) collective-permute-start(f32[10,32,256]{2,1,0:T(8,128)S(1)} %slice_dynamic-update-slice_fusion.refs_1_), channel_id=1, source_target_pairs={{0,24},{1,7},{2,26},{3,1},{4,28},{5,3},{6,30},{7,5},{8,0},{9,15},{... | collective-permute-start | bytes 983048 | tf_op jit(solution)/shard_map/ppermute | solution.py:39
  99.6 7.2 %collective-permute-done.20.refs_2_ = f32[10,32,256]{2,1,0:T(8,128)S(1)} collective-permute-done((f32[10,32,256]{2,1,0:T(8,128)S(1)}, f32[10,32,256]{2,1,0:T(8,128)S(1)}, u32[]{:S(2)}, u32[]{:S(2)}) %collective-permute-start.20) | collective-permute-done | bytes 327712 | tf_op jit(solution)/shard_map/ppermute | solution.py:39
  106.9 0.5 collective-permute-start.25
  107.4 0.4 collective-permute-done.22.refs_4_
  108.5 0.5 collective-permute-done.25.refs_7_
  109.0 0.5 collective-permute-done.26.refs_8_
  109.4 22.4 %solve.1 = (f32[1024,128]{1,0:T(8,128)}, f32[32,1024]{1,0:T(8,128)S(1)}, f32[32,1024]{1,0:T(8,128)S(1)}, f32[32,1024]{1,0:T(8,128)S(1)}, f32[32,1024]{1,0:T(8,128)S(1)}, /*index=5*/f32[128,128]{1,0:T(8,128)S(1)}) custom-call(s32[1]{0:T(128)S(6)} %copy.31.refs_0_, f32[10,32,256]{2,1,0:T(8,128)S(1)} %slice_dynamic-update-slice_fusion.refs_1_, ...), custom_call_target="tpu_custom_call" | custom-call | flops 8000000000 | bytes 9437184 | tf_op jit(solution)/shard_map/solve/pallas_call | solution.py:321
  132.1 1.1 collective-permute-done.30
  133.2 2.0 %collective-permute-start.33 = (f32[128,128]{1,0:T(8,128)S(1)}, f32[128,128]{1,0:T(8,128)S(1)}, u32[]{:S(2)}, u32[]{:S(2)}) collective-permute-start(f32[128,128]{1,0:T(8,128)S(1)} %add.234), channel_id=1, source_target_pairs={{0,16},{1,5},{2,18},{3,7},{4,20},{5,1},{6,22},{7,3},{8,24},{9,13},... | collective-permute-start | bytes 196616 | tf_op jit(solution)/shard_map/ppermute | solution.py:39
  135.1 2.0 %collective-permute-start.32 = (f32[128,128]{1,0:T(8,128)S(1)}, f32[128,128]{1,0:T(8,128)S(1)}, u32[]{:S(2)}, u32[]{:S(2)}) collective-permute-start(f32[128,128]{1,0:T(8,128)S(1)} %add.234), channel_id=1, source_target_pairs={{0,24},{1,7},{2,26},{3,1},{4,28},{5,3},{6,30},{7,5},{8,0},{9,15},{... | collective-permute-start | bytes 196616 | tf_op jit(solution)/shard_map/ppermute | solution.py:39
  137.2 1.9 %collective-permute-done.33 = f32[128,128]{1,0:T(8,128)S(1)} collective-permute-done((f32[128,128]{1,0:T(8,128)S(1)}, f32[128,128]{1,0:T(8,128)S(1)}, u32[]{:S(2)}, u32[]{:S(2)}) %collective-permute-start.33) | collective-permute-done | bytes 65568 | tf_op jit(solution)/shard_map/ppermute | solution.py:39
  139.0 0.6 collective-permute-done.32
  139.7 3.0 %collective-permute-done.31 = f32[128,128]{1,0:T(8,128)S(1)} collective-permute-done((f32[128,128]{1,0:T(8,128)S(1)}, f32[128,128]{1,0:T(8,128)S(1)}, u32[]{:S(2)}, u32[]{:S(2)}) %collective-permute-start.31) | collective-permute-done | bytes 65568 | tf_op jit(solution)/shard_map/ppermute | solution.py:39
  143.0 2.0 %collective-permute-start.35 = (f32[128,128]{1,0:T(8,128)S(1)}, f32[128,128]{1,0:T(8,128)S(1)}, u32[]{:S(2)}, u32[]{:S(2)}) collective-permute-start(f32[128,128]{1,0:T(8,128)S(1)} %add_add_fusion.3), channel_id=1, source_target_pairs={{0,6},{1,25},{2,0},{3,27},{4,2},{5,29},{6,4},{7,31},{8,14},{9,1},{... | collective-permute-start | bytes 196616 | tf_op jit(solution)/shard_map/ppermute | solution.py:39
  145.1 1.3 collective-permute-start.27
  146.4 2.4 %collective-permute-start.28 = (f32[32,1024]{1,0:T(8,128)S(1)}, f32[32,1024]{1,0:T(8,128)S(1)}, u32[]{:S(2)}, u32[]{:S(2)}) collective-permute-start(f32[32,1024]{1,0:T(8,128)S(1)} %get-tuple-element.44), channel_id=1, source_target_pairs={{0,64},{32,96},{64,0},{96,32},{1,65},{33,97},{65,1},{97,33},{2,66}... | collective-permute-start | bytes 393224 | tf_op jit(solution)/shard_map/ppermute | solution.py:22
  148.8 2.2 %collective-permute-start.29 = (f32[32,1024]{1,0:T(8,128)S(1)}, f32[32,1024]{1,0:T(8,128)S(1)}, u32[]{:S(2)}, u32[]{:S(2)}) collective-permute-start(f32[32,1024]{1,0:T(8,128)S(1)} %get-tuple-element.45), channel_id=1, source_target_pairs={{0,96},{32,0},{64,32},{96,64},{1,97},{33,1},{65,33},{97,65},{2,98}... | collective-permute-start | bytes 393224 | tf_op jit(solution)/shard_map/ppermute | solution.py:22
  151.0 1.7 %collective-permute-start.39 = (f32[128,128]{1,0:T(8,128)S(1)}, f32[128,128]{1,0:T(8,128)S(1)}, u32[]{:S(2)}, u32[]{:S(2)}) collective-permute-start(f32[128,128]{1,0:T(8,128)S(1)} %add_add_fusion.2), channel_id=1, source_target_pairs={{0,64},{32,96},{64,0},{96,32},{1,65},{33,97},{65,1},{97,33},{2,66}... | collective-permute-start | bytes 196616 | tf_op jit(solution)/shard_map/ppermute | solution.py:22
  152.7 1.8 %collective-permute-start.38 = (f32[128,128]{1,0:T(8,128)S(1)}, f32[128,128]{1,0:T(8,128)S(1)}, u32[]{:S(2)}, u32[]{:S(2)}) collective-permute-start(f32[128,128]{1,0:T(8,128)S(1)} %add_add_fusion.2), channel_id=1, source_target_pairs={{0,96},{32,0},{64,32},{96,64},{1,97},{33,1},{65,33},{97,65},{2,98}... | collective-permute-start | bytes 196616 | tf_op jit(solution)/shard_map/ppermute | solution.py:22
  154.9 0.8 join_columns.1
  155.8 1.1 collective-permute-done.39
  157.0 3.0 %collective-permute-done.37 = f32[128,128]{1,0:T(8,128)S(1)} collective-permute-done((f32[128,128]{1,0:T(8,128)S(1)}, f32[128,128]{1,0:T(8,128)S(1)}, u32[]{:S(2)}, u32[]{:S(2)}) %collective-permute-start.37) | collective-permute-done | bytes 65568 | tf_op jit(solution)/shard_map/ppermute | solution.py:22
  160.0 0.6 add_multiply_fusion
  (51 shorter events, 1.9 us)
Async XLA Ops:
  0.6 108.8 %copy-start.1 = (f32[1024,128]{1,0:T(8,128)S(1)}, f32[1024,128]{1,0:T(8,128)}, u32[]{:S(2)}) copy-start(f32[1024,128]{1,0:T(8,128)} %refs_9_.1) | copy-start | bytes 1572868
  3.6 26.5 %collective-permute-start = (f32[256,1024]{1,0:T(8,128)}, f32[256,1024]{1,0:T(8,128)S(1)}, u32[]{:S(2)}, u32[]{:S(2)}) collective-permute-start(f32[256,1024]{1,0:T(8,128)} %get-tuple-element.25), channel_id=1, source_target_pairs={{0,32},{32,64},{64,96},{96,0},{1,33},{33,65},{65,97},{97,1},{2,34}... | collective-permute-start | bytes 3145736 | tf_op jit(solution)/shard_map/ppermute | solution.py:22
  5.3 24.8 %collective-permute-start.1 = (f32[256,1024]{1,0:T(8,128)}, f32[256,1024]{1,0:T(8,128)S(1)}, u32[]{:S(2)}, u32[]{:S(2)}) collective-permute-start(f32[256,1024]{1,0:T(8,128)} %get-tuple-element.26), channel_id=1, source_target_pairs={{0,96},{32,0},{64,32},{96,64},{1,97},{33,1},{65,33},{97,65},{2,98}... | collective-permute-start | bytes 3145736 | tf_op jit(solution)/shard_map/ppermute | solution.py:22
  6.9 2.2 %copy-start = (f32[256,4096]{1,0:T(8,128)S(1)}, f32[256,4096]{1,0:T(8,128)}, u32[]{:S(2)}) copy-start(f32[256,4096]{1,0:T(8,128)} %slab.3) | copy-start | bytes 12582916
  30.2 25.7 %collective-permute-start.6 = (f32[256,1024]{1,0:T(8,128)S(1)}, f32[256,1024]{1,0:T(8,128)S(1)}, u32[]{:S(2)}, u32[]{:S(2)}) collective-permute-start(f32[256,1024]{1,0:T(8,128)S(1)} %get-tuple-element.35), channel_id=1, source_target_pairs={{0,64},{32,96},{64,0},{96,32},{1,65},{33,97},{65,1},{97,33},{2,66}... | collective-permute-start | bytes 3145736 | tf_op jit(solution)/shard_map/ppermute | solution.py:22
  36.4 2.3 %collective-permute-start.2 = (f32[4,128,256]{2,1,0:T(8,128)}, f32[4,128,256]{2,1,0:T(8,128)}, u32[]{:S(2)}, u32[]{:S(2)}) collective-permute-start(f32[4,128,256]{2,1,0:T(8,128)} %get-tuple-element.34), channel_id=1, source_target_pairs={{0,1},{1,0},{2,3},{3,2},{4,5},{5,4},{6,7},{7,6},{8,9},{9,8},{10,11... | collective-permute-start | bytes 1572872 | tf_op jit(solution)/shard_map/ppermute | solution.py:26
  39.9 0.8 copy-start.2
  40.7 6.6 %collective-permute-start.5 = (f32[4,32,256]{2,1,0:T(8,128)S(1)}, f32[4,32,256]{2,1,0:T(8,128)S(1)}, u32[]{:S(2)}, u32[]{:S(2)}) collective-permute-start(f32[4,32,256]{2,1,0:T(8,128)S(1)} %get-tuple-element.49), channel_id=1, source_target_pairs={{0,16},{1,5},{2,18},{3,7},{4,20},{5,1},{6,22},{7,3},{8,24},{9,13},... | collective-permute-start | bytes 393224 | tf_op jit(solution)/shard_map/ppermute | solution.py:39
  43.8 5.0 %collective-permute-start.4 = (f32[4,32,256]{2,1,0:T(8,128)S(1)}, f32[4,32,256]{2,1,0:T(8,128)S(1)}, u32[]{:S(2)}, u32[]{:S(2)}) collective-permute-start(f32[4,32,256]{2,1,0:T(8,128)S(1)} %get-tuple-element.48), channel_id=1, source_target_pairs={{0,24},{1,7},{2,26},{3,1},{4,28},{5,3},{6,30},{7,5},{8,0},{9,15},{... | collective-permute-start | bytes 393224 | tf_op jit(solution)/shard_map/ppermute | solution.py:39
  44.9 6.2 %collective-permute-start.3 = (f32[4,32,256]{2,1,0:T(8,128)S(1)}, f32[4,32,256]{2,1,0:T(8,128)S(1)}, u32[]{:S(2)}, u32[]{:S(2)}) collective-permute-start(f32[4,32,256]{2,1,0:T(8,128)S(1)} %get-tuple-element.47), channel_id=1, source_target_pairs={{0,8},{1,3},{2,10},{3,5},{4,12},{5,7},{6,14},{7,1},{8,16},{9,11},{... | collective-permute-start | bytes 393224 | tf_op jit(solution)/shard_map/ppermute | solution.py:39
  60.4 1.8 %collective-permute-start.10 = (f32[3,128,256]{2,1,0:T(8,128)S(1)}, f32[3,128,256]{2,1,0:T(8,128)S(1)}, u32[]{:S(2)}, u32[]{:S(2)}) collective-permute-start(f32[3,128,256]{2,1,0:T(8,128)S(1)} %get-tuple-element.40), channel_id=1, source_target_pairs={{0,1},{1,0},{2,3},{3,2},{4,5},{5,4},{6,7},{7,6},{8,9},{9,8},{10,11... | collective-permute-start | bytes 1179656 | tf_op jit(solution)/shard_map/ppermute | solution.py:26
  62.3 9.6 %collective-permute-start.13 = (f32[3,32,256]{2,1,0:T(8,128)S(1)}, f32[3,32,256]{2,1,0:T(8,128)S(1)}, u32[]{:S(2)}, u32[]{:S(2)}) collective-permute-start(f32[3,32,256]{2,1,0:T(8,128)S(1)} %get-tuple-element.52), channel_id=1, source_target_pairs={{0,16},{1,5},{2,18},{3,7},{4,20},{5,1},{6,22},{7,3},{8,24},{9,13},... | collective-permute-start | bytes 294920 | tf_op jit(solution)/shard_map/ppermute | solution.py:39
  65.3 7.9 %collective-permute-start.12 = (f32[3,32,256]{2,1,0:T(8,128)S(1)}, f32[3,32,256]{2,1,0:T(8,128)S(1)}, u32[]{:S(2)}, u32[]{:S(2)}) collective-permute-start(f32[3,32,256]{2,1,0:T(8,128)S(1)} %get-tuple-element.51), channel_id=1, source_target_pairs={{0,24},{1,7},{2,26},{3,1},{4,28},{5,3},{6,30},{7,5},{8,0},{9,15},{... | collective-permute-start | bytes 294920 | tf_op jit(solution)/shard_map/ppermute | solution.py:39
  66.4 7.2 %collective-permute-start.11 = (f32[3,32,256]{2,1,0:T(8,128)S(1)}, f32[3,32,256]{2,1,0:T(8,128)S(1)}, u32[]{:S(2)}, u32[]{:S(2)}) collective-permute-start(f32[3,32,256]{2,1,0:T(8,128)S(1)} %get-tuple-element.50), channel_id=1, source_target_pairs={{0,8},{1,3},{2,10},{3,5},{4,12},{5,7},{6,14},{7,1},{8,16},{9,11},{... | collective-permute-start | bytes 294920 | tf_op jit(solution)/shard_map/ppermute | solution.py:39
  67.3 10.5 %collective-permute-start.9 = (f32[4,32,256]{2,1,0:T(8,128)S(1)}, f32[4,32,256]{2,1,0:T(8,128)S(1)}, u32[]{:S(2)}, u32[]{:S(2)}) collective-permute-start(f32[4,32,256]{2,1,0:T(8,128)S(1)} %fusion.1), channel_id=1, source_target_pairs={{0,4},{1,17},{2,6},{3,19},{4,0},{5,21},{6,2},{7,23},{8,12},{9,25},... | collective-permute-start | bytes 393224 | tf_op jit(solution)/shard_map/ppermute | solution.py:39
  71.2 7.2 %collective-permute-start.8 = (f32[4,32,256]{2,1,0:T(8,128)S(1)}, f32[4,32,256]{2,1,0:T(8,128)S(1)}, u32[]{:S(2)}, u32[]{:S(2)}) collective-permute-start(f32[4,32,256]{2,1,0:T(8,128)S(1)} %fusion.1), channel_id=1, source_target_pairs={{0,6},{1,25},{2,0},{3,27},{4,2},{5,29},{6,4},{7,31},{8,14},{9,1},{... | collective-permute-start | bytes 393224 | tf_op jit(solution)/shard_map/ppermute | solution.py:39
  71.9 6.5 %collective-permute-start.7 = (f32[4,32,256]{2,1,0:T(8,128)S(1)}, f32[4,32,256]{2,1,0:T(8,128)S(1)}, u32[]{:S(2)}, u32[]{:S(2)}) collective-permute-start(f32[4,32,256]{2,1,0:T(8,128)S(1)} %fusion.1), channel_id=1, source_target_pairs={{0,2},{1,9},{2,4},{3,11},{4,6},{5,13},{6,0},{7,15},{8,10},{9,17},{... | collective-permute-start | bytes 393224 | tf_op jit(solution)/shard_map/ppermute | solution.py:39
  73.7 6.2 %collective-permute-start.16 = (f32[3,32,256]{2,1,0:T(8,128)S(1)}, f32[3,32,256]{2,1,0:T(8,128)S(1)}, u32[]{:S(2)}, u32[]{:S(2)}) collective-permute-start(f32[3,32,256]{2,1,0:T(8,128)S(1)} %fusion.3), channel_id=1, source_target_pairs={{0,4},{1,17},{2,6},{3,19},{4,0},{5,21},{6,2},{7,23},{8,12},{9,25},... | collective-permute-start | bytes 294920 | tf_op jit(solution)/shard_map/ppermute | solution.py:39
  76.4 5.0 %collective-permute-start.15 = (f32[3,32,256]{2,1,0:T(8,128)S(1)}, f32[3,32,256]{2,1,0:T(8,128)S(1)}, u32[]{:S(2)}, u32[]{:S(2)}) collective-permute-start(f32[3,32,256]{2,1,0:T(8,128)S(1)} %fusion.3), channel_id=1, source_target_pairs={{0,6},{1,25},{2,0},{3,27},{4,2},{5,29},{6,4},{7,31},{8,14},{9,1},{... | collective-permute-start | bytes 294920 | tf_op jit(solution)/shard_map/ppermute | solution.py:39
  77.8 5.8 %collective-permute-start.14 = (f32[3,32,256]{2,1,0:T(8,128)S(1)}, f32[3,32,256]{2,1,0:T(8,128)S(1)}, u32[]{:S(2)}, u32[]{:S(2)}) collective-permute-start(f32[3,32,256]{2,1,0:T(8,128)S(1)} %fusion.3), channel_id=1, source_target_pairs={{0,2},{1,9},{2,4},{3,11},{4,6},{5,13},{6,0},{7,15},{8,10},{9,17},{... | collective-permute-start | bytes 294920 | tf_op jit(solution)/shard_map/ppermute | solution.py:39
  83.7 8.7 %collective-permute-start.19 = (f32[7,32,256]{2,1,0:T(8,128)S(1)}, f32[7,32,256]{2,1,0:T(8,128)S(1)}, u32[]{:S(2)}, u32[]{:S(2)}) collective-permute-start(f32[7,32,256]{2,1,0:T(8,128)S(1)} %pad_maximum_fusion), channel_id=1, source_target_pairs={{0,32},{32,64},{64,96},{96,0},{1,33},{33,65},{65,97},{97,1},{2,34}... | collective-permute-start | bytes 688136 | tf_op jit(solution)/shard_map/ppermute | solution.py:22
  85.0 9.9 %collective-permute-start.18 = (f32[7,32,256]{2,1,0:T(8,128)S(1)}, f32[7,32,256]{2,1,0:T(8,128)S(1)}, u32[]{:S(2)}, u32[]{:S(2)}) collective-permute-start(f32[7,32,256]{2,1,0:T(8,128)S(1)} %pad_maximum_fusion), channel_id=1, source_target_pairs={{0,64},{32,96},{64,0},{96,32},{1,65},{33,97},{65,1},{97,33},{2,66}... | collective-permute-start | bytes 688136 | tf_op jit(solution)/shard_map/ppermute | solution.py:22
  88.0 6.8 %collective-permute-start.17 = (f32[7,32,256]{2,1,0:T(8,128)S(1)}, f32[7,32,256]{2,1,0:T(8,128)S(1)}, u32[]{:S(2)}, u32[]{:S(2)}) collective-permute-start(f32[7,32,256]{2,1,0:T(8,128)S(1)} %pad_maximum_fusion), channel_id=1, source_target_pairs={{0,96},{32,0},{64,32},{96,64},{1,97},{33,1},{65,33},{97,65},{2,98}... | collective-permute-start | bytes 688136 | tf_op jit(solution)/shard_map/ppermute | solution.py:22
  95.0 11.9 %collective-permute-start.20 = (f32[10,32,256]{2,1,0:T(8,128)S(1)}, f32[10,32,256]{2,1,0:T(8,128)S(1)}, u32[]{:S(2)}, u32[]{:S(2)}) collective-permute-start(f32[10,32,256]{2,1,0:T(8,128)S(1)} %slice_dynamic-update-slice_fusion.refs_1_), channel_id=1, source_target_pairs={{0,8},{1,3},{2,10},{3,5},{4,12},{5,7},{6,14},{7,1},{8,16},{9,11},{... | collective-permute-start | bytes 983048 | tf_op jit(solution)/shard_map/ppermute | solution.py:39
  95.9 11.0 %collective-permute-start.21 = (f32[10,32,256]{2,1,0:T(8,128)S(1)}, f32[10,32,256]{2,1,0:T(8,128)S(1)}, u32[]{:S(2)}, u32[]{:S(2)}) collective-permute-start(f32[10,32,256]{2,1,0:T(8,128)S(1)} %slice_dynamic-update-slice_fusion.refs_1_), channel_id=1, source_target_pairs={{0,16},{1,5},{2,18},{3,7},{4,20},{5,1},{6,22},{7,3},{8,24},{9,13},... | collective-permute-start | bytes 983048 | tf_op jit(solution)/shard_map/ppermute | solution.py:39
  97.7 10.0 %collective-permute-start.22 = (f32[10,32,256]{2,1,0:T(8,128)S(1)}, f32[10,32,256]{2,1,0:T(8,128)S(1)}, u32[]{:S(2)}, u32[]{:S(2)}) collective-permute-start(f32[10,32,256]{2,1,0:T(8,128)S(1)} %slice_dynamic-update-slice_fusion.refs_1_), channel_id=1, source_target_pairs={{0,24},{1,7},{2,26},{3,1},{4,28},{5,3},{6,30},{7,5},{8,0},{9,15},{... | collective-permute-start | bytes 983048 | tf_op jit(solution)/shard_map/ppermute | solution.py:39
  99.6 8.8 %collective-permute-start.23 = (f32[10,32,256]{2,1,0:T(8,128)S(1)}, f32[10,32,256]{2,1,0:T(8,128)S(1)}, u32[]{:S(2)}, u32[]{:S(2)}) collective-permute-start(f32[10,32,256]{2,1,0:T(8,128)S(1)} %slice_dynamic-update-slice_fusion.refs_1_), channel_id=1, source_target_pairs={{0,1},{1,0},{2,3},{3,2},{4,5},{5,4},{6,7},{7,6},{8,9},{9,8},{10,11... | collective-permute-start | bytes 983048 | tf_op jit(solution)/shard_map/ppermute | solution.py:26
  106.9 1.6 %collective-permute-start.24 = (f32[10,32,256]{2,1,0:T(8,128)S(1)}, f32[10,32,256]{2,1,0:T(8,128)S(1)}, u32[]{:S(2)}, u32[]{:S(2)}) collective-permute-start(f32[10,32,256]{2,1,0:T(8,128)S(1)} %collective-permute-done.20.refs_2_), channel_id=1, source_target_pairs={{0,1},{1,0},{2,3},{3,2},{4,5},{5,4},{6,7},{7,6},{8,9},{9,8},{10,11... | collective-permute-start | bytes 983048 | tf_op jit(solution)/shard_map/ppermute | solution.py:26
  106.9 2.1 %collective-permute-start.25 = (f32[10,32,256]{2,1,0:T(8,128)S(1)}, f32[10,32,256]{2,1,0:T(8,128)S(1)}, u32[]{:S(2)}, u32[]{:S(2)}) collective-permute-start(f32[10,32,256]{2,1,0:T(8,128)S(1)} %collective-permute-done.21.refs_3_), channel_id=1, source_target_pairs={{0,1},{1,0},{2,3},{3,2},{4,5},{5,4},{6,7},{7,6},{8,9},{9,8},{10,11... | collective-permute-start | bytes 983048 | tf_op jit(solution)/shard_map/ppermute | solution.py:26
  107.8 1.7 %collective-permute-start.26 = (f32[10,32,256]{2,1,0:T(8,128)S(1)}, f32[10,32,256]{2,1,0:T(8,128)S(1)}, u32[]{:S(2)}, u32[]{:S(2)}) collective-permute-start(f32[10,32,256]{2,1,0:T(8,128)S(1)} %collective-permute-done.22.refs_4_), channel_id=1, source_target_pairs={{0,1},{1,0},{2,3},{3,2},{4,5},{5,4},{6,7},{7,6},{8,9},{9,8},{10,11... | collective-permute-start | bytes 983048 | tf_op jit(solution)/shard_map/ppermute | solution.py:26
  131.8 1.3 collective-permute-start.30
  133.2 5.8 %collective-permute-start.33 = (f32[128,128]{1,0:T(8,128)S(1)}, f32[128,128]{1,0:T(8,128)S(1)}, u32[]{:S(2)}, u32[]{:S(2)}) collective-permute-start(f32[128,128]{1,0:T(8,128)S(1)} %add.234), channel_id=1, source_target_pairs={{0,16},{1,5},{2,18},{3,7},{4,20},{5,1},{6,22},{7,3},{8,24},{9,13},... | collective-permute-start | bytes 196616 | tf_op jit(solution)/shard_map/ppermute | solution.py:39
  135.1 4.5 %collective-permute-start.32 = (f32[128,128]{1,0:T(8,128)S(1)}, f32[128,128]{1,0:T(8,128)S(1)}, u32[]{:S(2)}, u32[]{:S(2)}) collective-permute-start(f32[128,128]{1,0:T(8,128)S(1)} %add.234), channel_id=1, source_target_pairs={{0,24},{1,7},{2,26},{3,1},{4,28},{5,3},{6,30},{7,5},{8,0},{9,15},{... | collective-permute-start | bytes 196616 | tf_op jit(solution)/shard_map/ppermute | solution.py:39
  137.2 5.5 %collective-permute-start.31 = (f32[128,128]{1,0:T(8,128)S(1)}, f32[128,128]{1,0:T(8,128)S(1)}, u32[]{:S(2)}, u32[]{:S(2)}) collective-permute-start(f32[128,128]{1,0:T(8,128)S(1)} %add.234), channel_id=1, source_target_pairs={{0,8},{1,3},{2,10},{3,5},{4,12},{5,7},{6,14},{7,1},{8,16},{9,11},{... | collective-permute-start | bytes 196616 | tf_op jit(solution)/shard_map/ppermute | solution.py:39
  142.7 6.1 %collective-permute-start.36 = (f32[128,128]{1,0:T(8,128)S(1)}, f32[128,128]{1,0:T(8,128)S(1)}, u32[]{:S(2)}, u32[]{:S(2)}) collective-permute-start(f32[128,128]{1,0:T(8,128)S(1)} %add_add_fusion.3), channel_id=1, source_target_pairs={{0,4},{1,17},{2,6},{3,19},{4,0},{5,21},{6,2},{7,23},{8,12},{9,25},... | collective-permute-start | bytes 196616 | tf_op jit(solution)/shard_map/ppermute | solution.py:39
  143.0 8.0 %collective-permute-start.35 = (f32[128,128]{1,0:T(8,128)S(1)}, f32[128,128]{1,0:T(8,128)S(1)}, u32[]{:S(2)}, u32[]{:S(2)}) collective-permute-start(f32[128,128]{1,0:T(8,128)S(1)} %add_add_fusion.3), channel_id=1, source_target_pairs={{0,6},{1,25},{2,0},{3,27},{4,2},{5,29},{6,4},{7,31},{8,14},{9,1},{... | collective-permute-start | bytes 196616 | tf_op jit(solution)/shard_map/ppermute | solution.py:39
  145.0 6.0 %collective-permute-start.34 = (f32[128,128]{1,0:T(8,128)S(1)}, f32[128,128]{1,0:T(8,128)S(1)}, u32[]{:S(2)}, u32[]{:S(2)}) collective-permute-start(f32[128,128]{1,0:T(8,128)S(1)} %add_add_fusion.3), channel_id=1, source_target_pairs={{0,2},{1,9},{2,4},{3,11},{4,6},{5,13},{6,0},{7,15},{8,10},{9,17},{... | collective-permute-start | bytes 196616 | tf_op jit(solution)/shard_map/ppermute | solution.py:39
  145.1 9.4 %collective-permute-start.27 = (f32[32,1024]{1,0:T(8,128)S(1)}, f32[32,1024]{1,0:T(8,128)S(1)}, u32[]{:S(2)}, u32[]{:S(2)}) collective-permute-start(f32[32,1024]{1,0:T(8,128)S(1)} %get-tuple-element.43), channel_id=1, source_target_pairs={{0,32},{32,64},{64,96},{96,0},{1,33},{33,65},{65,97},{97,1},{2,34}... | collective-permute-start | bytes 393224 | tf_op jit(solution)/shard_map/ppermute | solution.py:22
  146.4 8.4 %collective-permute-start.28 = (f32[32,1024]{1,0:T(8,128)S(1)}, f32[32,1024]{1,0:T(8,128)S(1)}, u32[]{:S(2)}, u32[]{:S(2)}) collective-permute-start(f32[32,1024]{1,0:T(8,128)S(1)} %get-tuple-element.44), channel_id=1, source_target_pairs={{0,64},{32,96},{64,0},{96,32},{1,65},{33,97},{65,1},{97,33},{2,66}... | collective-permute-start | bytes 393224 | tf_op jit(solution)/shard_map/ppermute | solution.py:22
  148.8 6.2 %collective-permute-start.29 = (f32[32,1024]{1,0:T(8,128)S(1)}, f32[32,1024]{1,0:T(8,128)S(1)}, u32[]{:S(2)}, u32[]{:S(2)}) collective-permute-start(f32[32,1024]{1,0:T(8,128)S(1)} %get-tuple-element.45), channel_id=1, source_target_pairs={{0,96},{32,0},{64,32},{96,64},{1,97},{33,1},{65,33},{97,65},{2,98}... | collective-permute-start | bytes 393224 | tf_op jit(solution)/shard_map/ppermute | solution.py:22
  151.0 5.8 %collective-permute-start.39 = (f32[128,128]{1,0:T(8,128)S(1)}, f32[128,128]{1,0:T(8,128)S(1)}, u32[]{:S(2)}, u32[]{:S(2)}) collective-permute-start(f32[128,128]{1,0:T(8,128)S(1)} %add_add_fusion.2), channel_id=1, source_target_pairs={{0,64},{32,96},{64,0},{96,32},{1,65},{33,97},{65,1},{97,33},{2,66}... | collective-permute-start | bytes 196616 | tf_op jit(solution)/shard_map/ppermute | solution.py:22
  152.7 4.3 %collective-permute-start.38 = (f32[128,128]{1,0:T(8,128)S(1)}, f32[128,128]{1,0:T(8,128)S(1)}, u32[]{:S(2)}, u32[]{:S(2)}) collective-permute-start(f32[128,128]{1,0:T(8,128)S(1)} %add_add_fusion.2), channel_id=1, source_target_pairs={{0,96},{32,0},{64,32},{96,64},{1,97},{33,1},{65,33},{97,65},{2,98}... | collective-permute-start | bytes 196616 | tf_op jit(solution)/shard_map/ppermute | solution.py:22
  154.5 5.5 %collective-permute-start.37 = (f32[128,128]{1,0:T(8,128)S(1)}, f32[128,128]{1,0:T(8,128)S(1)}, u32[]{:S(2)}, u32[]{:S(2)}) collective-permute-start(f32[128,128]{1,0:T(8,128)S(1)} %add_add_fusion.2), channel_id=1, source_target_pairs={{0,32},{32,64},{64,96},{96,0},{1,33},{33,65},{65,97},{97,1},{2,34}... | collective-permute-start | bytes 196616 | tf_op jit(solution)/shard_map/ppermute | solution.py:22
where the time goes:
time: 161 us
  waiting for transfers between devices  61.8 us (38%)
  starting transfers between devices  53.7 us (33%)
  Pallas kernels  37.4 us (23%)
  local copies, waits for them, and re-layouts  3.06 us (2%)
  other arithmetic  2.97 us (2%)
  between operations  1.61 us (1%)
    ppermute x12, waiting for transfers between devices, along_y(): return lax.ppermute(v, 'tm', [(i, (i + k) % NY) for i in range(NY)])  31.8 us
    ppermute x21, starting transfers between devices, along_xz(): return lax.ppermute(v, 'rest', perm)  31.8 us
    ppermute x21, waiting for transfers between devices, along_xz(): return lax.ppermute(v, 'rest', perm)  24 us
    pallas_call x1, Pallas kernels, solve(): pl.pallas_call(body, out_shape=(struct((time_all, ranks), F32), part, par...  22.4 us
    ppermute x12, starting transfers between devices, along_y(): return lax.ppermute(v, 'tm', [(i, (i + k) % NY) for i in range(NY)])  21 us
    pallas_call x3, Pallas kernels, gram_call(): pl.pallas_call(kernel, out_shape=[half, half] + [struct((2, rows, cols) i...  11.2 us
    ppermute x7, waiting for transfers between devices, along_core(): return lax.ppermute(v, 'rest', [(i, i ^ 1) for i in range(2 * NX * NZ)])  5.99 us
  transfers between devices with their start and end apart: 40, of which 26 were waited for; matrix products, arithmetic and copies ran while one was open for 1% of the time, Pallas kernels for 5%

commit v1 on v0

--- a/solution.py
+++ b/solution.py
@@ -96,14 +96,21 @@
         out.wait()
 
 
-def slices_kernel(slab, ahead, behind, sem):
+def slices_kernel(slab, ahead, behind, held, sem):
     me_y = lax.axis_index("tm")
     width = ahead.shape[1]
-    outs = []
+    rows = held.shape[2]
+    ins, outs = [], []
     for n, (k, out) in enumerate(((1, ahead), (3, behind))):
         at = pl.ds(pl.multiple_of(around(me_y, k) * width, 128), width)
-        outs.append(pltpu.make_async_copy(slab.at[:, at], out, sem.at[n]))
-    for out in outs:
+        for r in range(held.shape[1]):
+            part = pl.ds(r * rows, rows)
+            ins.append(pltpu.make_async_copy(slab.at[part, at], held.at[n, r], sem.at[0, n, r]))
+            outs.append(pltpu.make_async_copy(held.at[n, r], out.at[part, :], sem.at[1, n, r]))
+    for copy in ins:
+        copy.start()
+    for copy, out in zip(ins, outs):
+        copy.wait()
         out.start()
     for out in outs:
         out.wait()
@@ -112,12 +119,16 @@
 def slices(slab):
     out = jax.ShapeDtypeStruct((slab.shape[0], slab.shape[1] // NY), F32)
     hbm = pl.BlockSpec(memory_space=HBM)
+    parts = 4
     return pl.pallas_call(
         slices_kernel,
         out_shape=[out, out],
         in_specs=[hbm],
-        out_specs=[pl.BlockSpec(memory_space=VMEM)] * 2,
-        scratch_shapes=[pltpu.SemaphoreType.DMA((2,))],
+        out_specs=[hbm, hbm],
+        scratch_shapes=[
+            VMEM((2, parts, out.shape[0] // parts, out.shape[1]), F32),
+            pltpu.SemaphoreType.DMA((2, 2, parts)),
+        ],
         compiler_params=pltpu.CompilerParams(vmem_limit_bytes=56 * 2**20),
         name="slices",
     )(slab)
@@ -170,6 +181,14 @@
         cost_estimate=pl.CostEstimate(flops=COST.get(name, 10**9), bytes_accessed=1000, transcendentals=0),
         name=name,
     )(*vmem_args, *hbm_args)
+
+
+def chain(pairs, ca, cb):
+    total = None
+    for a, b in pairs:
+        term = dot(a, b, ca, cb)
+        total = term if total is None else total + term
+    return total
 
 
 def row_of(v, k):
@@ -224,9 +243,11 @@
         if p > first and first + 4 < panels:
             h, m, l = split3(jnp.concatenate([jnp.concatenate([left[t], right[t]], 1) for t in (first, p)], 0))
             lh, lm, ll = h[:, :n], m[:, :n], l[:, :n]
-            update = dot(jnp.concatenate([lh, lh, lm, lm, lh, ll], 0), jnp.concatenate([h, m, h, m, l, h], 0), 0, 0)
             start = 8 * (first + 4)
-            work[start:, :] = work[start:, :] - update[start:]
+            a = jnp.concatenate([lh, lh, lm, lm, lh, ll], 0)
+            b = jnp.concatenate([h, m, h, m, l, h], 0)
+            update = dot(a.T[start:], b, 1, 0)
+            work[start:, :] = work[start:, :] - update
         column = ahead
     return jnp.concatenate([right[p] for p in range(panels)], 0)
 
@@ -262,14 +283,14 @@
 
     def step(_, carry):
         h, m, l = split3(iterate[...])
-        by_h = dot(jnp.concatenate([h, m, l], 0), gh[...].reshape(NY * t, NY * t), 1, 0)
-        by_m = dot(jnp.concatenate([h, m], 0), gm[...].reshape(NY * t, NY * t), 1, 0)
-        by_l = dot(h, gl[...].reshape(NY * t, NY * t), 1, 0)
-        image = by_h[:n] + ((by_h[n : 2 * n] + by_m[:n]) + (by_h[2 * n :] + by_m[n:] + by_l))
+        wide = [g[...].reshape(NY * t, NY * t) for g in (gh, gm, gl)]
+        image = dot(h, wide[0], 1, 0) + (
+            (dot(m, wide[0], 1, 0) + dot(h, wide[1], 1, 0))
+            + (dot(l, wide[0], 1, 0) + dot(m, wide[1], 1, 0) + dot(h, wide[2], 1, 0))
+        )
         h, m, l = split3(image)
-        by_h = dot(jnp.concatenate([h, m, l], 0), h, 1, 1)
-        small = by_h[n : 2 * n] + by_h[2 * n :]
-        work[:, :n] = by_h[:n] + ((small + small.T) + dot(m, m, 1, 1))
+        small = dot(l, h, 1, 1) + dot(m, h, 1, 1)
+        work[:, :n] = dot(h, h, 1, 1) + ((small + small.T) + dot(m, m, 1, 1))
         ih, im, il = split3(cholesky_inverse(work))
         by_h = dot(jnp.concatenate([ih, im, il], 0), h, 1, 0)
         by_m = dot(jnp.concatenate([ih, im], 0), m, 1, 0)
@@ -289,8 +310,7 @@
             hl[2, 0], hl[2, 1] = split2(last[...])
         at = pl.ds(pl.multiple_of(around(me_y, d) * t, t), t)
         hs, ls = qhl[0, :, at], qhl[1, :, at]
-        by_hi = dot(jnp.concatenate([hs, ls], 0), hl[d, 0], 1, 0)
-        term = by_hi[:n] + (by_hi[n:] + dot(hs, hl[d, 1], 1, 0))
+        term = dot(hs, hl[d, 0], 1, 0) + (dot(ls, hl[d, 0], 1, 0) + dot(hs, hl[d, 1], 1, 0))
         total = term if total is None else total + term
     core[...] = total
     own = n // NY

time: 161 us -> 158 us (0.981)
  Pallas kernels: 37.4 us -> 34.5 us
    pallas_call x1, Pallas kernels: 22.4 us -> 20 us  [solve(): pl.pallas_call(body, out_shape=(struct((time_all, ranks), F32), part, par...]
where the time goes in v1:
time: 158 us
  waiting for transfers between devices  61.8 us (39%)
  starting transfers between devices  53.8 us (34%)
  Pallas kernels  34.5 us (22%)
  local copies, waits for them, and re-layouts  3.06 us (2%)
  other arithmetic  2.97 us (2%)
  between operations  1.61 us (1%)
    ppermute x21, starting transfers between devices, along_xz(): return lax.ppermute(v, 'rest', perm)  31.8 us
    ppermute x12, waiting for transfers between devices, along_y(): return lax.ppermute(v, 'tm', [(i, (i + k) % NY) for i in range(NY)])  31.8 us
    ppermute x21, waiting for transfers between devices, along_xz(): return lax.ppermute(v, 'rest', perm)  24 us
    ppermute x12, starting transfers between devices, along_y(): return lax.ppermute(v, 'tm', [(i, (i + k) % NY) for i in range(NY)])  21.1 us
    pallas_call x1, Pallas kernels, solve(): pl.pallas_call(body, out_shape=(struct((time_all, ranks), F32), part, par...  20 us
    pallas_call x3, Pallas kernels, gram_call(): pl.pallas_call(kernel, out_shape=[half, half] + [struct((2, rows, cols) i...  11.2 us
    ppermute x7, waiting for transfers between devices, along_core(): return lax.ppermute(v, 'rest', [(i, i ^ 1) for i in range(2 * NX * NZ)])  5.99 us
  transfers between devices with their start and end apart: 40, of which 26 were waited for; matrix products, arithmetic and copies ran while one was open for 1% of the time, Pallas kernels for 5%

profile of v1, /device:TPU:0, one launch (start us, length us, event | category | flops | bytes accessed | tf_op | source)
XLA Modules:
  0.0 157.8 jit_solution(2887473338050887071)
XLA Ops:
  0.6 2.5 %slices.1 = (f32[256,1024]{1,0:T(8,128)}, f32[256,1024]{1,0:T(8,128)}) custom-call(f32[256,4096]{1,0:T(8,128)} %slab.3), custom_call_target="tpu_custom_call" | custom-call | tf_op jit(solution)/shard_map/slices/pallas_call | solution.py:123
  3.1 1.7 %collective-permute-start = (f32[256,1024]{1,0:T(8,128)}, f32[256,1024]{1,0:T(8,128)S(1)}, u32[]{:S(2)}, u32[]{:S(2)}) collective-permute-start(f32[256,1024]{1,0:T(8,128)} %get-tuple-element.25), channel_id=1, source_target_pairs={{0,32},{32,64},{64,96},{96,0},{1,33},{33,65},{65,97},{97,1},{2,34}... | collective-permute-start | bytes 3145736 | tf_op jit(solution)/shard_map/ppermute | solution.py:22
  4.9 1.6 collective-permute-start.1
  6.4 2.2 %copy-done = f32[256,4096]{1,0:T(8,128)S(1)} copy-done((f32[256,4096]{1,0:T(8,128)S(1)}, f32[256,4096]{1,0:T(8,128)}, u32[]{:S(2)}) %copy-start) | copy-done | bytes 4194328
  8.6 3.4 %own_gram.1 = (f32[128,256]{1,0:T(8,128)S(1)}, f32[128,256]{1,0:T(8,128)S(1)}, bf16[2,256,1024]{2,1,0:T(8,128)(2,1)S(1)}, f32[256,1024]{1,0:T(8,128)S(1)}) custom-call(f32[256,4096]{1,0:T(8,128)S(1)} %copy-done), custom_call_target="tpu_custom_call" | custom-call | flops 1000000000 | bytes 1000 | tf_op jit(solution)/shard_map/own_gram/pallas_call | solution.py:174
  12.0 17.7 %collective-permute-done.w1 = f32[256,1024]{1,0:T(8,128)S(1)} collective-permute-done((f32[256,1024]{1,0:T(8,128)}, f32[256,1024]{1,0:T(8,128)S(1)}, u32[]{:S(2)}, u32[]{:S(2)}) %collective-permute-start) | collective-permute-done | bytes 1048608 | tf_op jit(solution)/shard_map/ppermute | solution.py:22
  29.7 2.9 %collective-permute-start.6 = (f32[256,1024]{1,0:T(8,128)S(1)}, f32[256,1024]{1,0:T(8,128)S(1)}, u32[]{:S(2)}, u32[]{:S(2)}) collective-permute-start(f32[256,1024]{1,0:T(8,128)S(1)} %get-tuple-element.35), channel_id=1, source_target_pairs={{0,64},{32,96},{64,0},{96,32},{1,65},{33,97},{65,1},{97,33},{2,66}... | collective-permute-start | bytes 3145736 | tf_op jit(solution)/shard_map/ppermute | solution.py:22
  32.6 3.3 %early_gram.1 = (f32[4,128,256]{2,1,0:T(8,128)}, f32[4,128,256]{2,1,0:T(8,128)S(1)}, bf16[56,2,256,1024]{3,2,1,0:T(8,128)(2,1)}) custom-call(f32[256,1024]{1,0:T(8,128)S(1)} %collective-permute-done.w1, f32[256,1024]{1,0:T(8,128)S(1)} %collective-permute-done.1.w3, f32[128,256]{1,0:T(8,128)S(1)} %get-tuple-element.30.send0, ...), custom_call_target="tpu_custom_call" | custom-call | flops 1000000000 | bytes 1000 | tf_op jit(solution)/shard_map/early_gram/pallas_call | solution.py:174
  36.1 2.2 %collective-permute-done.2 = f32[4,128,256]{2,1,0:T(8,128)} collective-permute-done((f32[4,128,256]{2,1,0:T(8,128)}, f32[4,128,256]{2,1,0:T(8,128)}, u32[]{:S(2)}, u32[]{:S(2)}) %collective-permute-start.2) | collective-permute-done | bytes 524320 | tf_op jit(solution)/shard_map/ppermute | solution.py:26
  38.3 1.1 add.191
  39.4 0.8 copy-done.2
  40.2 3.1 %collective-permute-start.5 = (f32[4,32,256]{2,1,0:T(8,128)S(1)}, f32[4,32,256]{2,1,0:T(8,128)S(1)}, u32[]{:S(2)}, u32[]{:S(2)}) collective-permute-start(f32[4,32,256]{2,1,0:T(8,128)S(1)} %get-tuple-element.49), channel_id=1, source_target_pairs={{0,16},{1,5},{2,18},{3,7},{4,20},{5,1},{6,22},{7,3},{8,24},{9,13},... | collective-permute-start | bytes 393224 | tf_op jit(solution)/shard_map/ppermute | solution.py:39
  43.3 1.1 collective-permute-start.4
  44.5 0.9 collective-permute-start.3
  45.4 1.4 collective-permute-done.5
  46.8 1.5 collective-permute-done.4
  48.3 2.3 %collective-permute-done.3 = f32[4,32,256]{2,1,0:T(8,128)S(1)} collective-permute-done((f32[4,32,256]{2,1,0:T(8,128)S(1)}, f32[4,32,256]{2,1,0:T(8,128)S(1)}, u32[]{:S(2)}, u32[]{:S(2)}) %collective-permute-start.3) | collective-permute-done | bytes 131104 | tf_op jit(solution)/shard_map/ppermute | solution.py:39
  50.6 0.9 fusion.1
  51.6 3.8 %collective-permute-done.6.w2.refs_11_ = f32[256,1024]{1,0:T(8,128)S(1)} collective-permute-done((f32[256,1024]{1,0:T(8,128)S(1)}, f32[256,1024]{1,0:T(8,128)S(1)}, u32[]{:S(2)}, u32[]{:S(2)}) %collective-permute-start.6) | collective-permute-done | bytes 1048608 | tf_op jit(solution)/shard_map/ppermute | solution.py:22
  55.4 4.5 %late_gram.1 = (f32[3,128,256]{2,1,0:T(8,128)S(1)}, f32[3,128,256]{2,1,0:T(8,128)S(1)}) custom-call(f32[256,1024]{1,0:T(8,128)S(1)} %collective-permute-done.6.w2.refs_11_, bf16[56,2,256,1024]{3,2,1,0:T(8,128)(2,1)} %get-tuple-element.38.hls.refs_10_), custom_call_target="tpu_custom_call" | custom-call | flops 20000000000 | bytes 1000 | tf_op jit(solution)/shard_map/late_gram/pallas_call | solution.py:174
  60.0 1.7 %collective-permute-done.10 = f32[3,128,256]{2,1,0:T(8,128)S(1)} collective-permute-done((f32[3,128,256]{2,1,0:T(8,128)S(1)}, f32[3,128,256]{2,1,0:T(8,128)S(1)}, u32[]{:S(2)}, u32[]{:S(2)}) %collective-permute-start.10) | collective-permute-done | bytes 393248 | tf_op jit(solution)/shard_map/ppermute | solution.py:26
  61.8 3.0 %collective-permute-start.13 = (f32[3,32,256]{2,1,0:T(8,128)S(1)}, f32[3,32,256]{2,1,0:T(8,128)S(1)}, u32[]{:S(2)}, u32[]{:S(2)}) collective-permute-start(f32[3,32,256]{2,1,0:T(8,128)S(1)} %get-tuple-element.52), channel_id=1, source_target_pairs={{0,16},{1,5},{2,18},{3,7},{4,20},{5,1},{6,22},{7,3},{8,24},{9,13},... | collective-permute-start | bytes 294920 | tf_op jit(solution)/shard_map/ppermute | solution.py:39
  64.8 1.1 collective-permute-start.12
  66.0 0.9 collective-permute-start.11
  66.8 3.9 %collective-permute-start.9 = (f32[4,32,256]{2,1,0:T(8,128)S(1)}, f32[4,32,256]{2,1,0:T(8,128)S(1)}, u32[]{:S(2)}, u32[]{:S(2)}) collective-permute-start(f32[4,32,256]{2,1,0:T(8,128)S(1)} %fusion.1), channel_id=1, source_target_pairs={{0,4},{1,17},{2,6},{3,19},{4,0},{5,21},{6,2},{7,23},{8,12},{9,25},... | collective-permute-start | bytes 393224 | tf_op jit(solution)/shard_map/ppermute | solution.py:39
  70.7 0.7 collective-permute-start.8
  71.4 1.3 collective-permute-start.7
  72.8 0.4 collective-permute-done.11
  73.2 2.7 %collective-permute-start.16 = (f32[3,32,256]{2,1,0:T(8,128)S(1)}, f32[3,32,256]{2,1,0:T(8,128)S(1)}, u32[]{:S(2)}, u32[]{:S(2)}) collective-permute-start(f32[3,32,256]{2,1,0:T(8,128)S(1)} %fusion.3), channel_id=1, source_target_pairs={{0,4},{1,17},{2,6},{3,19},{4,0},{5,21},{6,2},{7,23},{8,12},{9,25},... | collective-permute-start | bytes 294920 | tf_op jit(solution)/shard_map/ppermute | solution.py:39
  75.9 1.4 collective-permute-start.15
  77.4 0.6 collective-permute-start.14
  78.0 1.4 collective-permute-done.16
  79.4 1.5 collective-permute-done.15
  80.9 2.2 %collective-permute-done.14 = f32[3,32,256]{2,1,0:T(8,128)S(1)} collective-permute-done((f32[3,32,256]{2,1,0:T(8,128)S(1)}, f32[3,32,256]{2,1,0:T(8,128)S(1)}, u32[]{:S(2)}, u32[]{:S(2)}) %collective-permute-start.14) | collective-permute-done | bytes 98336 | tf_op jit(solution)/shard_map/ppermute | solution.py:39
  83.2 1.3 collective-permute-start.19
  84.5 3.0 %collective-permute-start.18 = (f32[7,32,256]{2,1,0:T(8,128)S(1)}, f32[7,32,256]{2,1,0:T(8,128)S(1)}, u32[]{:S(2)}, u32[]{:S(2)}) collective-permute-start(f32[7,32,256]{2,1,0:T(8,128)S(1)} %pad_maximum_fusion), channel_id=1, source_target_pairs={{0,64},{32,96},{64,0},{96,32},{1,65},{33,97},{65,1},{97,33},{2,66}... | collective-permute-start | bytes 688136 | tf_op jit(solution)/shard_map/ppermute | solution.py:22
  87.6 0.9 collective-permute-start.17
  88.5 3.4 %collective-permute-done.19 = f32[7,32,256]{2,1,0:T(8,128)S(1)} collective-permute-done((f32[7,32,256]{2,1,0:T(8,128)S(1)}, f32[7,32,256]{2,1,0:T(8,128)S(1)}, u32[]{:S(2)}, u32[]{:S(2)}) %collective-permute-start.19) | collective-permute-done | bytes 229408 | tf_op jit(solution)/shard_map/ppermute | solution.py:22
  91.9 2.5 %collective-permute-done.18 = f32[7,32,256]{2,1,0:T(8,128)S(1)} collective-permute-done((f32[7,32,256]{2,1,0:T(8,128)S(1)}, f32[7,32,256]{2,1,0:T(8,128)S(1)}, u32[]{:S(2)}, u32[]{:S(2)}) %collective-permute-start.18) | collective-permute-done | bytes 229408 | tf_op jit(solution)/shard_map/ppermute | solution.py:22
  94.5 0.9 collective-permute-start.20
  95.4 1.9 %collective-permute-start.21 = (f32[10,32,256]{2,1,0:T(8,128)S(1)}, f32[10,32,256]{2,1,0:T(8,128)S(1)}, u32[]{:S(2)}, u32[]{:S(2)}) collective-permute-start(f32[10,32,256]{2,1,0:T(8,128)S(1)} %slice_dynamic-update-slice_fusion.refs_1_), channel_id=1, source_target_pairs={{0,16},{1,5},{2,18},{3,7},{4,20},{5,1},{6,22},{7,3},{8,24},{9,13},... | collective-permute-start | bytes 983048 | tf_op jit(solution)/shard_map/ppermute | solution.py:39
  97.3 1.9 %collective-permute-start.22 = (f32[10,32,256]{2,1,0:T(8,128)S(1)}, f32[10,32,256]{2,1,0:T(8,128)S(1)}, u32[]{:S(2)}, u32[]{:S(2)}) collective-permute-start(f32[10,32,256]{2,1,0:T(8,128)S(1)} %slice_dynamic-update-slice_fusion.refs_1_), channel_id=1, source_target_pairs={{0,24},{1,7},{2,26},{3,1},{4,28},{5,3},{6,30},{7,5},{8,0},{9,15},{... | collective-permute-start | bytes 983048 | tf_op jit(solution)/shard_map/ppermute | solution.py:39
  99.1 7.2 %collective-permute-done.20.refs_2_ = f32[10,32,256]{2,1,0:T(8,128)S(1)} collective-permute-done((f32[10,32,256]{2,1,0:T(8,128)S(1)}, f32[10,32,256]{2,1,0:T(8,128)S(1)}, u32[]{:S(2)}, u32[]{:S(2)}) %collective-permute-start.20) | collective-permute-done | bytes 327712 | tf_op jit(solution)/shard_map/ppermute | solution.py:39
  106.4 0.5 collective-permute-start.25
  106.9 0.4 collective-permute-done.22.refs_4_
  108.0 0.5 collective-permute-done.25.refs_7_
  108.5 0.5 collective-permute-done.26.refs_8_
  109.0 20.0 %solve.1 = (f32[1024,128]{1,0:T(8,128)}, f32[32,1024]{1,0:T(8,128)S(1)}, f32[32,1024]{1,0:T(8,128)S(1)}, f32[32,1024]{1,0:T(8,128)S(1)}, f32[32,1024]{1,0:T(8,128)S(1)}, /*index=5*/f32[128,128]{1,0:T(8,128)S(1)}) custom-call(s32[1]{0:T(128)S(6)} %copy.31.refs_0_, f32[10,32,256]{2,1,0:T(8,128)S(1)} %slice_dynamic-update-slice_fusion.refs_1_, ...), custom_call_target="tpu_custom_call" | custom-call | flops 8000000000 | bytes 9437184 | tf_op jit(solution)/shard_map/solve/pallas_call | solution.py:341
  129.2 1.1 collective-permute-done.30
  130.3 2.0 %collective-permute-start.33 = (f32[128,128]{1,0:T(8,128)S(1)}, f32[128,128]{1,0:T(8,128)S(1)}, u32[]{:S(2)}, u32[]{:S(2)}) collective-permute-start(f32[128,128]{1,0:T(8,128)S(1)} %add.234), channel_id=1, source_target_pairs={{0,16},{1,5},{2,18},{3,7},{4,20},{5,1},{6,22},{7,3},{8,24},{9,13},... | collective-permute-start | bytes 196616 | tf_op jit(solution)/shard_map/ppermute | solution.py:39
  132.3 2.0 %collective-permute-start.32 = (f32[128,128]{1,0:T(8,128)S(1)}, f32[128,128]{1,0:T(8,128)S(1)}, u32[]{:S(2)}, u32[]{:S(2)}) collective-permute-start(f32[128,128]{1,0:T(8,128)S(1)} %add.234), channel_id=1, source_target_pairs={{0,24},{1,7},{2,26},{3,1},{4,28},{5,3},{6,30},{7,5},{8,0},{9,15},{... | collective-permute-start | bytes 196616 | tf_op jit(solution)/shard_map/ppermute | solution.py:39
  134.3 1.9 %collective-permute-done.33 = f32[128,128]{1,0:T(8,128)S(1)} collective-permute-done((f32[128,128]{1,0:T(8,128)S(1)}, f32[128,128]{1,0:T(8,128)S(1)}, u32[]{:S(2)}, u32[]{:S(2)}) %collective-permute-start.33) | collective-permute-done | bytes 65568 | tf_op jit(solution)/shard_map/ppermute | solution.py:39
  136.2 0.6 collective-permute-done.32
  136.8 3.0 %collective-permute-done.31 = f32[128,128]{1,0:T(8,128)S(1)} collective-permute-done((f32[128,128]{1,0:T(8,128)S(1)}, f32[128,128]{1,0:T(8,128)S(1)}, u32[]{:S(2)}, u32[]{:S(2)}) %collective-permute-start.31) | collective-permute-done | bytes 65568 | tf_op jit(solution)/shard_map/ppermute | solution.py:39
  140.1 2.0 %collective-permute-start.35 = (f32[128,128]{1,0:T(8,128)S(1)}, f32[128,128]{1,0:T(8,128)S(1)}, u32[]{:S(2)}, u32[]{:S(2)}) collective-permute-start(f32[128,128]{1,0:T(8,128)S(1)} %add_add_fusion.3), channel_id=1, source_target_pairs={{0,6},{1,25},{2,0},{3,27},{4,2},{5,29},{6,4},{7,31},{8,14},{9,1},{... | collective-permute-start | bytes 196616 | tf_op jit(solution)/shard_map/ppermute | solution.py:39
  142.2 1.3 collective-permute-start.27
  143.5 2.4 %collective-permute-start.28 = (f32[32,1024]{1,0:T(8,128)S(1)}, f32[32,1024]{1,0:T(8,128)S(1)}, u32[]{:S(2)}, u32[]{:S(2)}) collective-permute-start(f32[32,1024]{1,0:T(8,128)S(1)} %get-tuple-element.44), channel_id=1, source_target_pairs={{0,64},{32,96},{64,0},{96,32},{1,65},{33,97},{65,1},{97,33},{2,66}... | collective-permute-start | bytes 393224 | tf_op jit(solution)/shard_map/ppermute | solution.py:22
  145.9 2.2 %collective-permute-start.29 = (f32[32,1024]{1,0:T(8,128)S(1)}, f32[32,1024]{1,0:T(8,128)S(1)}, u32[]{:S(2)}, u32[]{:S(2)}) collective-permute-start(f32[32,1024]{1,0:T(8,128)S(1)} %get-tuple-element.45), channel_id=1, source_target_pairs={{0,96},{32,0},{64,32},{96,64},{1,97},{33,1},{65,33},{97,65},{2,98}... | collective-permute-start | bytes 393224 | tf_op jit(solution)/shard_map/ppermute | solution.py:22
  148.1 1.7 %collective-permute-start.39 = (f32[128,128]{1,0:T(8,128)S(1)}, f32[128,128]{1,0:T(8,128)S(1)}, u32[]{:S(2)}, u32[]{:S(2)}) collective-permute-start(f32[128,128]{1,0:T(8,128)S(1)} %add_add_fusion.2), channel_id=1, source_target_pairs={{0,64},{32,96},{64,0},{96,32},{1,65},{33,97},{65,1},{97,33},{2,66}... | collective-permute-start | bytes 196616 | tf_op jit(solution)/shard_map/ppermute | solution.py:22
  149.8 1.8 %collective-permute-start.38 = (f32[128,128]{1,0:T(8,128)S(1)}, f32[128,128]{1,0:T(8,128)S(1)}, u32[]{:S(2)}, u32[]{:S(2)}) collective-permute-start(f32[128,128]{1,0:T(8,128)S(1)} %add_add_fusion.2), channel_id=1, source_target_pairs={{0,96},{32,0},{64,32},{96,64},{1,97},{33,1},{65,33},{97,65},{2,98}... | collective-permute-start | bytes 196616 | tf_op jit(solution)/shard_map/ppermute | solution.py:22
  152.0 0.8 join_columns.1
  152.9 1.1 collective-permute-done.39
  154.1 3.0 %collective-permute-done.37 = f32[128,128]{1,0:T(8,128)S(1)} collective-permute-done((f32[128,128]{1,0:T(8,128)S(1)}, f32[128,128]{1,0:T(8,128)S(1)}, u32[]{:S(2)}, u32[]{:S(2)}) %collective-permute-start.37) | collective-permute-done | bytes 65568 | tf_op jit(solution)/shard_map/ppermute | solution.py:22
  157.1 0.6 add_multiply_fusion
  (51 shorter events, 1.8 us)
Async XLA Ops:
  0.6 108.3 %copy-start.1 = (f32[1024,128]{1,0:T(8,128)S(1)}, f32[1024,128]{1,0:T(8,128)}, u32[]{:S(2)}) copy-start(f32[1024,128]{1,0:T(8,128)} %refs_9_.1) | copy-start | bytes 1572868
  3.1 26.5 %collective-permute-start = (f32[256,1024]{1,0:T(8,128)}, f32[256,1024]{1,0:T(8,128)S(1)}, u32[]{:S(2)}, u32[]{:S(2)}) collective-permute-start(f32[256,1024]{1,0:T(8,128)} %get-tuple-element.25), channel_id=1, source_target_pairs={{0,32},{32,64},{64,96},{96,0},{1,33},{33,65},{65,97},{97,1},{2,34}... | collective-permute-start | bytes 3145736 | tf_op jit(solution)/shard_map/ppermute | solution.py:22
  4.9 24.8 %collective-permute-start.1 = (f32[256,1024]{1,0:T(8,128)}, f32[256,1024]{1,0:T(8,128)S(1)}, u32[]{:S(2)}, u32[]{:S(2)}) collective-permute-start(f32[256,1024]{1,0:T(8,128)} %get-tuple-element.26), channel_id=1, source_target_pairs={{0,96},{32,0},{64,32},{96,64},{1,97},{33,1},{65,33},{97,65},{2,98}... | collective-permute-start | bytes 3145736 | tf_op jit(solution)/shard_map/ppermute | solution.py:22
  6.4 2.2 %copy-start = (f32[256,4096]{1,0:T(8,128)S(1)}, f32[256,4096]{1,0:T(8,128)}, u32[]{:S(2)}) copy-start(f32[256,4096]{1,0:T(8,128)} %slab.3) | copy-start | bytes 12582916
  29.7 25.7 %collective-permute-start.6 = (f32[256,1024]{1,0:T(8,128)S(1)}, f32[256,1024]{1,0:T(8,128)S(1)}, u32[]{:S(2)}, u32[]{:S(2)}) collective-permute-start(f32[256,1024]{1,0:T(8,128)S(1)} %get-tuple-element.35), channel_id=1, source_target_pairs={{0,64},{32,96},{64,0},{96,32},{1,65},{33,97},{65,1},{97,33},{2,66}... | collective-permute-start | bytes 3145736 | tf_op jit(solution)/shard_map/ppermute | solution.py:22
  35.9 2.3 %collective-permute-start.2 = (f32[4,128,256]{2,1,0:T(8,128)}, f32[4,128,256]{2,1,0:T(8,128)}, u32[]{:S(2)}, u32[]{:S(2)}) collective-permute-start(f32[4,128,256]{2,1,0:T(8,128)} %get-tuple-element.34), channel_id=1, source_target_pairs={{0,1},{1,0},{2,3},{3,2},{4,5},{5,4},{6,7},{7,6},{8,9},{9,8},{10,11... | collective-permute-start | bytes 1572872 | tf_op jit(solution)/shard_map/ppermute | solution.py:26
  39.4 0.8 copy-start.2
  40.2 6.6 %collective-permute-start.5 = (f32[4,32,256]{2,1,0:T(8,128)S(1)}, f32[4,32,256]{2,1,0:T(8,128)S(1)}, u32[]{:S(2)}, u32[]{:S(2)}) collective-permute-start(f32[4,32,256]{2,1,0:T(8,128)S(1)} %get-tuple-element.49), channel_id=1, source_target_pairs={{0,16},{1,5},{2,18},{3,7},{4,20},{5,1},{6,22},{7,3},{8,24},{9,13},... | collective-permute-start | bytes 393224 | tf_op jit(solution)/shard_map/ppermute | solution.py:39
  43.3 5.0 %collective-permute-start.4 = (f32[4,32,256]{2,1,0:T(8,128)S(1)}, f32[4,32,256]{2,1,0:T(8,128)S(1)}, u32[]{:S(2)}, u32[]{:S(2)}) collective-permute-start(f32[4,32,256]{2,1,0:T(8,128)S(1)} %get-tuple-element.48), channel_id=1, source_target_pairs={{0,24},{1,7},{2,26},{3,1},{4,28},{5,3},{6,30},{7,5},{8,0},{9,15},{... | collective-permute-start | bytes 393224 | tf_op jit(solution)/shard_map/ppermute | solution.py:39
  44.5 6.2 %collective-permute-start.3 = (f32[4,32,256]{2,1,0:T(8,128)S(1)}, f32[4,32,256]{2,1,0:T(8,128)S(1)}, u32[]{:S(2)}, u32[]{:S(2)}) collective-permute-start(f32[4,32,256]{2,1,0:T(8,128)S(1)} %get-tuple-element.47), channel_id=1, source_target_pairs={{0,8},{1,3},{2,10},{3,5},{4,12},{5,7},{6,14},{7,1},{8,16},{9,11},{... | collective-permute-start | bytes 393224 | tf_op jit(solution)/shard_map/ppermute | solution.py:39
  59.9 1.8 %collective-permute-start.10 = (f32[3,128,256]{2,1,0:T(8,128)S(1)}, f32[3,128,256]{2,1,0:T(8,128)S(1)}, u32[]{:S(2)}, u32[]{:S(2)}) collective-permute-start(f32[3,128,256]{2,1,0:T(8,128)S(1)} %get-tuple-element.40), channel_id=1, source_target_pairs={{0,1},{1,0},{2,3},{3,2},{4,5},{5,4},{6,7},{7,6},{8,9},{9,8},{10,11... | collective-permute-start | bytes 1179656 | tf_op jit(solution)/shard_map/ppermute | solution.py:26
  61.8 9.6 %collective-permute-start.13 = (f32[3,32,256]{2,1,0:T(8,128)S(1)}, f32[3,32,256]{2,1,0:T(8,128)S(1)}, u32[]{:S(2)}, u32[]{:S(2)}) collective-permute-start(f32[3,32,256]{2,1,0:T(8,128)S(1)} %get-tuple-element.52), channel_id=1, source_target_pairs={{0,16},{1,5},{2,18},{3,7},{4,20},{5,1},{6,22},{7,3},{8,24},{9,13},... | collective-permute-start | bytes 294920 | tf_op jit(solution)/shard_map/ppermute | solution.py:39
  64.8 7.9 %collective-permute-start.12 = (f32[3,32,256]{2,1,0:T(8,128)S(1)}, f32[3,32,256]{2,1,0:T(8,128)S(1)}, u32[]{:S(2)}, u32[]{:S(2)}) collective-permute-start(f32[3,32,256]{2,1,0:T(8,128)S(1)} %get-tuple-element.51), channel_id=1, source_target_pairs={{0,24},{1,7},{2,26},{3,1},{4,28},{5,3},{6,30},{7,5},{8,0},{9,15},{... | collective-permute-start | bytes 294920 | tf_op jit(solution)/shard_map/ppermute | solution.py:39
  66.0 7.2 %collective-permute-start.11 = (f32[3,32,256]{2,1,0:T(8,128)S(1)}, f32[3,32,256]{2,1,0:T(8,128)S(1)}, u32[]{:S(2)}, u32[]{:S(2)}) collective-permute-start(f32[3,32,256]{2,1,0:T(8,128)S(1)} %get-tuple-element.50), channel_id=1, source_target_pairs={{0,8},{1,3},{2,10},{3,5},{4,12},{5,7},{6,14},{7,1},{8,16},{9,11},{... | collective-permute-start | bytes 294920 | tf_op jit(solution)/shard_map/ppermute | solution.py:39
  66.8 10.5 %collective-permute-start.9 = (f32[4,32,256]{2,1,0:T(8,128)S(1)}, f32[4,32,256]{2,1,0:T(8,128)S(1)}, u32[]{:S(2)}, u32[]{:S(2)}) collective-permute-start(f32[4,32,256]{2,1,0:T(8,128)S(1)} %fusion.1), channel_id=1, source_target_pairs={{0,4},{1,17},{2,6},{3,19},{4,0},{5,21},{6,2},{7,23},{8,12},{9,25},... | collective-permute-start | bytes 393224 | tf_op jit(solution)/shard_map/ppermute | solution.py:39
  70.7 7.2 %collective-permute-start.8 = (f32[4,32,256]{2,1,0:T(8,128)S(1)}, f32[4,32,256]{2,1,0:T(8,128)S(1)}, u32[]{:S(2)}, u32[]{:S(2)}) collective-permute-start(f32[4,32,256]{2,1,0:T(8,128)S(1)} %fusion.1), channel_id=1, source_target_pairs={{0,6},{1,25},{2,0},{3,27},{4,2},{5,29},{6,4},{7,31},{8,14},{9,1},{... | collective-permute-start | bytes 393224 | tf_op jit(solution)/shard_map/ppermute | solution.py:39
  71.4 6.5 %collective-permute-start.7 = (f32[4,32,256]{2,1,0:T(8,128)S(1)}, f32[4,32,256]{2,1,0:T(8,128)S(1)}, u32[]{:S(2)}, u32[]{:S(2)}) collective-permute-start(f32[4,32,256]{2,1,0:T(8,128)S(1)} %fusion.1), channel_id=1, source_target_pairs={{0,2},{1,9},{2,4},{3,11},{4,6},{5,13},{6,0},{7,15},{8,10},{9,17},{... | collective-permute-start | bytes 393224 | tf_op jit(solution)/shard_map/ppermute | solution.py:39
  73.2 6.2 %collective-permute-start.16 = (f32[3,32,256]{2,1,0:T(8,128)S(1)}, f32[3,32,256]{2,1,0:T(8,128)S(1)}, u32[]{:S(2)}, u32[]{:S(2)}) collective-permute-start(f32[3,32,256]{2,1,0:T(8,128)S(1)} %fusion.3), channel_id=1, source_target_pairs={{0,4},{1,17},{2,6},{3,19},{4,0},{5,21},{6,2},{7,23},{8,12},{9,25},... | collective-permute-start | bytes 294920 | tf_op jit(solution)/shard_map/ppermute | solution.py:39
  75.9 5.0 %collective-permute-start.15 = (f32[3,32,256]{2,1,0:T(8,128)S(1)}, f32[3,32,256]{2,1,0:T(8,128)S(1)}, u32[]{:S(2)}, u32[]{:S(2)}) collective-permute-start(f32[3,32,256]{2,1,0:T(8,128)S(1)} %fusion.3), channel_id=1, source_target_pairs={{0,6},{1,25},{2,0},{3,27},{4,2},{5,29},{6,4},{7,31},{8,14},{9,1},{... | collective-permute-start | bytes 294920 | tf_op jit(solution)/shard_map/ppermute | solution.py:39
  77.4 5.8 %collective-permute-start.14 = (f32[3,32,256]{2,1,0:T(8,128)S(1)}, f32[3,32,256]{2,1,0:T(8,128)S(1)}, u32[]{:S(2)}, u32[]{:S(2)}) collective-permute-start(f32[3,32,256]{2,1,0:T(8,128)S(1)} %fusion.3), channel_id=1, source_target_pairs={{0,2},{1,9},{2,4},{3,11},{4,6},{5,13},{6,0},{7,15},{8,10},{9,17},{... | collective-permute-start | bytes 294920 | tf_op jit(solution)/shard_map/ppermute | solution.py:39
  83.2 8.7 %collective-permute-start.19 = (f32[7,32,256]{2,1,0:T(8,128)S(1)}, f32[7,32,256]{2,1,0:T(8,128)S(1)}, u32[]{:S(2)}, u32[]{:S(2)}) collective-permute-start(f32[7,32,256]{2,1,0:T(8,128)S(1)} %pad_maximum_fusion), channel_id=1, source_target_pairs={{0,32},{32,64},{64,96},{96,0},{1,33},{33,65},{65,97},{97,1},{2,34}... | collective-permute-start | bytes 688136 | tf_op jit(solution)/shard_map/ppermute | solution.py:22
  84.5 9.8 %collective-permute-start.18 = (f32[7,32,256]{2,1,0:T(8,128)S(1)}, f32[7,32,256]{2,1,0:T(8,128)S(1)}, u32[]{:S(2)}, u32[]{:S(2)}) collective-permute-start(f32[7,32,256]{2,1,0:T(8,128)S(1)} %pad_maximum_fusion), channel_id=1, source_target_pairs={{0,64},{32,96},{64,0},{96,32},{1,65},{33,97},{65,1},{97,33},{2,66}... | collective-permute-start | bytes 688136 | tf_op jit(solution)/shard_map/ppermute | solution.py:22
  87.6 6.8 %collective-permute-start.17 = (f32[7,32,256]{2,1,0:T(8,128)S(1)}, f32[7,32,256]{2,1,0:T(8,128)S(1)}, u32[]{:S(2)}, u32[]{:S(2)}) collective-permute-start(f32[7,32,256]{2,1,0:T(8,128)S(1)} %pad_maximum_fusion), channel_id=1, source_target_pairs={{0,96},{32,0},{64,32},{96,64},{1,97},{33,1},{65,33},{97,65},{2,98}... | collective-permute-start | bytes 688136 | tf_op jit(solution)/shard_map/ppermute | solution.py:22
  94.5 11.9 %collective-permute-start.20 = (f32[10,32,256]{2,1,0:T(8,128)S(1)}, f32[10,32,256]{2,1,0:T(8,128)S(1)}, u32[]{:S(2)}, u32[]{:S(2)}) collective-permute-start(f32[10,32,256]{2,1,0:T(8,128)S(1)} %slice_dynamic-update-slice_fusion.refs_1_), channel_id=1, source_target_pairs={{0,8},{1,3},{2,10},{3,5},{4,12},{5,7},{6,14},{7,1},{8,16},{9,11},{... | collective-permute-start | bytes 983048 | tf_op jit(solution)/shard_map/ppermute | solution.py:39
  95.4 11.0 %collective-permute-start.21 = (f32[10,32,256]{2,1,0:T(8,128)S(1)}, f32[10,32,256]{2,1,0:T(8,128)S(1)}, u32[]{:S(2)}, u32[]{:S(2)}) collective-permute-start(f32[10,32,256]{2,1,0:T(8,128)S(1)} %slice_dynamic-update-slice_fusion.refs_1_), channel_id=1, source_target_pairs={{0,16},{1,5},{2,18},{3,7},{4,20},{5,1},{6,22},{7,3},{8,24},{9,13},... | collective-permute-start | bytes 983048 | tf_op jit(solution)/shard_map/ppermute | solution.py:39
  97.3 10.0 %collective-permute-start.22 = (f32[10,32,256]{2,1,0:T(8,128)S(1)}, f32[10,32,256]{2,1,0:T(8,128)S(1)}, u32[]{:S(2)}, u32[]{:S(2)}) collective-permute-start(f32[10,32,256]{2,1,0:T(8,128)S(1)} %slice_dynamic-update-slice_fusion.refs_1_), channel_id=1, source_target_pairs={{0,24},{1,7},{2,26},{3,1},{4,28},{5,3},{6,30},{7,5},{8,0},{9,15},{... | collective-permute-start | bytes 983048 | tf_op jit(solution)/shard_map/ppermute | solution.py:39
  99.1 8.8 %collective-permute-start.23 = (f32[10,32,256]{2,1,0:T(8,128)S(1)}, f32[10,32,256]{2,1,0:T(8,128)S(1)}, u32[]{:S(2)}, u32[]{:S(2)}) collective-permute-start(f32[10,32,256]{2,1,0:T(8,128)S(1)} %slice_dynamic-update-slice_fusion.refs_1_), channel_id=1, source_target_pairs={{0,1},{1,0},{2,3},{3,2},{4,5},{5,4},{6,7},{7,6},{8,9},{9,8},{10,11... | collective-permute-start | bytes 983048 | tf_op jit(solution)/shard_map/ppermute | solution.py:26
  106.4 1.6 %collective-permute-start.24 = (f32[10,32,256]{2,1,0:T(8,128)S(1)}, f32[10,32,256]{2,1,0:T(8,128)S(1)}, u32[]{:S(2)}, u32[]{:S(2)}) collective-permute-start(f32[10,32,256]{2,1,0:T(8,128)S(1)} %collective-permute-done.20.refs_2_), channel_id=1, source_target_pairs={{0,1},{1,0},{2,3},{3,2},{4,5},{5,4},{6,7},{7,6},{8,9},{9,8},{10,11... | collective-permute-start | bytes 983048 | tf_op jit(solution)/shard_map/ppermute | solution.py:26
  106.4 2.1 %collective-permute-start.25 = (f32[10,32,256]{2,1,0:T(8,128)S(1)}, f32[10,32,256]{2,1,0:T(8,128)S(1)}, u32[]{:S(2)}, u32[]{:S(2)}) collective-permute-start(f32[10,32,256]{2,1,0:T(8,128)S(1)} %collective-permute-done.21.refs_3_), channel_id=1, source_target_pairs={{0,1},{1,0},{2,3},{3,2},{4,5},{5,4},{6,7},{7,6},{8,9},{9,8},{10,11... | collective-permute-start | bytes 983048 | tf_op jit(solution)/shard_map/ppermute | solution.py:26
  107.3 1.7 %collective-permute-start.26 = (f32[10,32,256]{2,1,0:T(8,128)S(1)}, f32[10,32,256]{2,1,0:T(8,128)S(1)}, u32[]{:S(2)}, u32[]{:S(2)}) collective-permute-start(f32[10,32,256]{2,1,0:T(8,128)S(1)} %collective-permute-done.22.refs_4_), channel_id=1, source_target_pairs={{0,1},{1,0},{2,3},{3,2},{4,5},{5,4},{6,7},{7,6},{8,9},{9,8},{10,11... | collective-permute-start | bytes 983048 | tf_op jit(solution)/shard_map/ppermute | solution.py:26
  129.0 1.3 collective-permute-start.30
  130.3 5.8 %collective-permute-start.33 = (f32[128,128]{1,0:T(8,128)S(1)}, f32[128,128]{1,0:T(8,128)S(1)}, u32[]{:S(2)}, u32[]{:S(2)}) collective-permute-start(f32[128,128]{1,0:T(8,128)S(1)} %add.234), channel_id=1, source_target_pairs={{0,16},{1,5},{2,18},{3,7},{4,20},{5,1},{6,22},{7,3},{8,24},{9,13},... | collective-permute-start | bytes 196616 | tf_op jit(solution)/shard_map/ppermute | solution.py:39
  132.3 4.5 %collective-permute-start.32 = (f32[128,128]{1,0:T(8,128)S(1)}, f32[128,128]{1,0:T(8,128)S(1)}, u32[]{:S(2)}, u32[]{:S(2)}) collective-permute-start(f32[128,128]{1,0:T(8,128)S(1)} %add.234), channel_id=1, source_target_pairs={{0,24},{1,7},{2,26},{3,1},{4,28},{5,3},{6,30},{7,5},{8,0},{9,15},{... | collective-permute-start | bytes 196616 | tf_op jit(solution)/shard_map/ppermute | solution.py:39
  134.3 5.5 %collective-permute-start.31 = (f32[128,128]{1,0:T(8,128)S(1)}, f32[128,128]{1,0:T(8,128)S(1)}, u32[]{:S(2)}, u32[]{:S(2)}) collective-permute-start(f32[128,128]{1,0:T(8,128)S(1)} %add.234), channel_id=1, source_target_pairs={{0,8},{1,3},{2,10},{3,5},{4,12},{5,7},{6,14},{7,1},{8,16},{9,11},{... | collective-permute-start | bytes 196616 | tf_op jit(solution)/shard_map/ppermute | solution.py:39
  139.8 6.1 %collective-permute-start.36 = (f32[128,128]{1,0:T(8,128)S(1)}, f32[128,128]{1,0:T(8,128)S(1)}, u32[]{:S(2)}, u32[]{:S(2)}) collective-permute-start(f32[128,128]{1,0:T(8,128)S(1)} %add_add_fusion.3), channel_id=1, source_target_pairs={{0,4},{1,17},{2,6},{3,19},{4,0},{5,21},{6,2},{7,23},{8,12},{9,25},... | collective-permute-start | bytes 196616 | tf_op jit(solution)/shard_map/ppermute | solution.py:39
  140.1 8.0 %collective-permute-start.35 = (f32[128,128]{1,0:T(8,128)S(1)}, f32[128,128]{1,0:T(8,128)S(1)}, u32[]{:S(2)}, u32[]{:S(2)}) collective-permute-start(f32[128,128]{1,0:T(8,128)S(1)} %add_add_fusion.3), channel_id=1, source_target_pairs={{0,6},{1,25},{2,0},{3,27},{4,2},{5,29},{6,4},{7,31},{8,14},{9,1},{... | collective-permute-start | bytes 196616 | tf_op jit(solution)/shard_map/ppermute | solution.py:39
  142.1 6.0 %collective-permute-start.34 = (f32[128,128]{1,0:T(8,128)S(1)}, f32[128,128]{1,0:T(8,128)S(1)}, u32[]{:S(2)}, u32[]{:S(2)}) collective-permute-start(f32[128,128]{1,0:T(8,128)S(1)} %add_add_fusion.3), channel_id=1, source_target_pairs={{0,2},{1,9},{2,4},{3,11},{4,6},{5,13},{6,0},{7,15},{8,10},{9,17},{... | collective-permute-start | bytes 196616 | tf_op jit(solution)/shard_map/ppermute | solution.py:39
  142.2 9.4 %collective-permute-start.27 = (f32[32,1024]{1,0:T(8,128)S(1)}, f32[32,1024]{1,0:T(8,128)S(1)}, u32[]{:S(2)}, u32[]{:S(2)}) collective-permute-start(f32[32,1024]{1,0:T(8,128)S(1)} %get-tuple-element.43), channel_id=1, source_target_pairs={{0,32},{32,64},{64,96},{96,0},{1,33},{33,65},{65,97},{97,1},{2,34}... | collective-permute-start | bytes 393224 | tf_op jit(solution)/shard_map/ppermute | solution.py:22
  143.5 8.4 %collective-permute-start.28 = (f32[32,1024]{1,0:T(8,128)S(1)}, f32[32,1024]{1,0:T(8,128)S(1)}, u32[]{:S(2)}, u32[]{:S(2)}) collective-permute-start(f32[32,1024]{1,0:T(8,128)S(1)} %get-tuple-element.44), channel_id=1, source_target_pairs={{0,64},{32,96},{64,0},{96,32},{1,65},{33,97},{65,1},{97,33},{2,66}... | collective-permute-start | bytes 393224 | tf_op jit(solution)/shard_map/ppermute | solution.py:22
  145.9 6.1 %collective-permute-start.29 = (f32[32,1024]{1,0:T(8,128)S(1)}, f32[32,1024]{1,0:T(8,128)S(1)}, u32[]{:S(2)}, u32[]{:S(2)}) collective-permute-start(f32[32,1024]{1,0:T(8,128)S(1)} %get-tuple-element.45), channel_id=1, source_target_pairs={{0,96},{32,0},{64,32},{96,64},{1,97},{33,1},{65,33},{97,65},{2,98}... | collective-permute-start | bytes 393224 | tf_op jit(solution)/shard_map/ppermute | solution.py:22
  148.1 5.8 %collective-permute-start.39 = (f32[128,128]{1,0:T(8,128)S(1)}, f32[128,128]{1,0:T(8,128)S(1)}, u32[]{:S(2)}, u32[]{:S(2)}) collective-permute-start(f32[128,128]{1,0:T(8,128)S(1)} %add_add_fusion.2), channel_id=1, source_target_pairs={{0,64},{32,96},{64,0},{96,32},{1,65},{33,97},{65,1},{97,33},{2,66}... | collective-permute-start | bytes 196616 | tf_op jit(solution)/shard_map/ppermute | solution.py:22
  149.8 4.3 %collective-permute-start.38 = (f32[128,128]{1,0:T(8,128)S(1)}, f32[128,128]{1,0:T(8,128)S(1)}, u32[]{:S(2)}, u32[]{:S(2)}) collective-permute-start(f32[128,128]{1,0:T(8,128)S(1)} %add_add_fusion.2), channel_id=1, source_target_pairs={{0,96},{32,0},{64,32},{96,64},{1,97},{33,1},{65,33},{97,65},{2,98}... | collective-permute-start | bytes 196616 | tf_op jit(solution)/shard_map/ppermute | solution.py:22
  151.6 5.5 %collective-permute-start.37 = (f32[128,128]{1,0:T(8,128)S(1)}, f32[128,128]{1,0:T(8,128)S(1)}, u32[]{:S(2)}, u32[]{:S(2)}) collective-permute-start(f32[128,128]{1,0:T(8,128)S(1)} %add_add_fusion.2), channel_id=1, source_target_pairs={{0,32},{32,64},{64,96},{96,0},{1,33},{33,65},{65,97},{97,1},{2,34}... | collective-permute-start | bytes 196616 | tf_op jit(solution)/shard_map/ppermute | solution.py:22

commit v2 on v1

--- a/solution.py
+++ b/solution.py
@@ -252,6 +252,52 @@
     return jnp.concatenate([right[p] for p in range(panels)], 0)
 
 
+def swap_halves(v):
+    half = v.shape[1] // 2
+    return jnp.concatenate([v[:, half:], v[:, :half]], 1)
+
+
+def places(shape):
+    return lax.broadcasted_iota(jnp.int32, shape, 0), lax.broadcasted_iota(jnp.int32, shape, 1)
+
+
+def pack_symmetric(v):
+    n = v.shape[0]
+    row, col = places((n // 2, n))
+    body = jnp.where(col >= row, v[: n // 2], swap_halves(v[n // 2 :]))
+    diagonal = jnp.sum(jnp.where(col == row + n // 2, v[n // 2 :], 0.0), 0, keepdims=True)
+    return jnp.concatenate([body, jnp.broadcast_to(diagonal, (8, n))], 0)
+
+
+def unpack_kernel(p0, p1, p2, p3, out, *, scale):
+    v = (p0[...] + p1[...] + p2[...] + p3[...]) * scale
+    n = v.shape[1]
+    body, diagonal = v[: n // 2], v[n // 2 : n // 2 + 1]
+    row, col = places((n // 2, n))
+    upper = jnp.where(col >= row, body, 0.0)
+    lower = jnp.where((col >= n // 2) & (col < row + n // 2), swap_halves(body), 0.0)
+    lower = jnp.where(col == row + n // 2, jnp.broadcast_to(diagonal, lower.shape), lower)
+    once = jnp.concatenate([upper, lower], 0)
+    row, col = places((n, n))
+    out[...] = once + jnp.where(row == col, 0.0, once.T)
+
+
+def unpack_sum(pieces, scale):
+    n = pieces[0].shape[1]
+
+    def body(*refs):
+        unpack_kernel(*refs, scale=scale)
+
+    return pl.pallas_call(
+        body,
+        out_shape=jax.ShapeDtypeStruct((n, n), F32),
+        in_specs=[pl.BlockSpec(memory_space=VMEM)] * 4,
+        out_specs=pl.BlockSpec(memory_space=VMEM),
+        compiler_params=pltpu.CompilerParams(vmem_limit_bytes=4 * 2**20),
+        name="unpack_sum",
+    )(*pieces)
+
+
 def solve_kernel(rank, *refs, scale):
     me_y, core_id, first, second = position()
     pieces, start, hls, w2 = refs[:8], refs[8], refs[9], refs[10]
@@ -322,7 +368,7 @@
         hs, ls = h[:, s * PARAMS : (s + 1) * PARAMS], l[:, s * PARAMS : (s + 1) * PARAMS]
         cross = dot(hs, ls, 0, 0)
         param = param + (dot(hs, hs, 0, 0) + (cross + cross.T) + dot(ls, ls, 0, 0))
-    param_out[...] = param
+    param_out[...] = pack_symmetric(param)
 
 
 def solve(rank, pieces, start_basis, hls, w2, scale):
@@ -340,7 +386,7 @@
 
     return pl.pallas_call(
         body,
-        out_shape=(struct((time_all, ranks), F32), part, part, part, part, struct((PARAMS, PARAMS), F32)),
+        out_shape=(struct((time_all, ranks), F32), part, part, part, part, struct((PARAMS // 2 + 8, PARAMS), F32)),
         in_specs=[smem] + [vmem] * 9 + [hbm] * 2,
         out_specs=[vmem] * 6,
         scratch_shapes=[
@@ -445,9 +491,8 @@
     param = param + along_core(param)
     param = exchange_sum(param, lambda u, k: along_xz(u, k, True))
     param = exchange_sum(param, lambda u, k: along_xz(u, k, False))
-    param = exchange_sum(param, along_y)
     space_all = columns_local // PARAMS * rest_count
-    param_gram = param / float(ranks * space_all)
+    param_gram = unpack_sum([param] + [along_y(param, k) for k in (1, 3, 2)], 1.0 / float(ranks * space_all))
 
     mine = {k: along_y(cores[k], k) for k in (1, 3, 2)}
     core = join_columns([cores[0], mine[1], mine[2], mine[3]])

time: 158 us -> 157 us (level)
  transfers between devices with their start and end apart: 40 -> 40, of which waited for: 26 -> 24; matrix products, arithmetic and copies ran while one was open for 1% -> 1% of each run, Pallas kernels for 5% -> 5%
where the time goes in v2:
time: 157 us
  waiting for transfers between devices  61.2 us (39%)
  starting transfers between devices  53.4 us (34%)
  Pallas kernels  35.3 us (22%)
  local copies, waits for them, and re-layouts  3.06 us (2%)
  other arithmetic  2.31 us (1%)
  between operations  1.6 us (1%)
    ppermute x21, starting transfers between devices, along_xz(): return lax.ppermute(v, 'rest', perm)  31.7 us
    ppermute x12, waiting for transfers between devices, along_y(): return lax.ppermute(v, 'tm', [(i, (i + k) % NY) for i in range(NY)])  31.6 us
    ppermute x21, waiting for transfers between devices, along_xz(): return lax.ppermute(v, 'rest', perm)  23.7 us
    ppermute x12, starting transfers between devices, along_y(): return lax.ppermute(v, 'tm', [(i, (i + k) % NY) for i in range(NY)])  20.8 us
    pallas_call x1, Pallas kernels, solve(): pl.pallas_call(body, out_shape=(struct((time_all, ranks), F32), part, par...  20 us
    pallas_call x3, Pallas kernels, gram_call(): pl.pallas_call(kernel, out_shape=[half, half] + [struct((2, rows, cols) i...  11.2 us
    ppermute x7, waiting for transfers between devices, along_core(): return lax.ppermute(v, 'rest', [(i, i ^ 1) for i in range(2 * NX * NZ)])  5.95 us
  transfers between devices with their start and end apart: 40, of which 24 were waited for; matrix products, arithmetic and copies ran while one was open for 1% of the time, Pallas kernels for 5%

profile of v2, /device:TPU:0, one launch (start us, length us, event | category | flops | bytes accessed | tf_op | source)
XLA Modules:
  0.0 156.9 jit_solution(9582949374626119613)
XLA Ops:
  0.6 2.5 %slices.1 = (f32[256,1024]{1,0:T(8,128)}, f32[256,1024]{1,0:T(8,128)}) custom-call(f32[256,4096]{1,0:T(8,128)} %slab.3), custom_call_target="tpu_custom_call" | custom-call | tf_op jit(solution)/shard_map/slices/pallas_call | solution.py:123
  3.1 1.7 %collective-permute-start = (f32[256,1024]{1,0:T(8,128)}, f32[256,1024]{1,0:T(8,128)S(1)}, u32[]{:S(2)}, u32[]{:S(2)}) collective-permute-start(f32[256,1024]{1,0:T(8,128)} %get-tuple-element.25), channel_id=1, source_target_pairs={{0,32},{32,64},{64,96},{96,0},{1,33},{33,65},{65,97},{97,1},{2,34}... | collective-permute-start | bytes 3145736 | tf_op jit(solution)/shard_map/ppermute | solution.py:22
  4.9 1.6 %collective-permute-start.1 = (f32[256,1024]{1,0:T(8,128)}, f32[256,1024]{1,0:T(8,128)S(1)}, u32[]{:S(2)}, u32[]{:S(2)}) collective-permute-start(f32[256,1024]{1,0:T(8,128)} %get-tuple-element.26), channel_id=1, source_target_pairs={{0,96},{32,0},{64,32},{96,64},{1,97},{33,1},{65,33},{97,65},{2,98}... | collective-permute-start | bytes 3145736 | tf_op jit(solution)/shard_map/ppermute | solution.py:22
  6.4 2.2 %copy-done = f32[256,4096]{1,0:T(8,128)S(1)} copy-done((f32[256,4096]{1,0:T(8,128)S(1)}, f32[256,4096]{1,0:T(8,128)}, u32[]{:S(2)}) %copy-start) | copy-done | bytes 4194328
  8.6 3.4 %own_gram.1 = (f32[128,256]{1,0:T(8,128)S(1)}, f32[128,256]{1,0:T(8,128)S(1)}, bf16[2,256,1024]{2,1,0:T(8,128)(2,1)S(1)}, f32[256,1024]{1,0:T(8,128)S(1)}) custom-call(f32[256,4096]{1,0:T(8,128)S(1)} %copy-done), custom_call_target="tpu_custom_call" | custom-call | flops 1000000000 | bytes 1000 | tf_op jit(solution)/shard_map/own_gram/pallas_call | solution.py:174
  12.0 17.7 %collective-permute-done.w1 = f32[256,1024]{1,0:T(8,128)S(1)} collective-permute-done((f32[256,1024]{1,0:T(8,128)}, f32[256,1024]{1,0:T(8,128)S(1)}, u32[]{:S(2)}, u32[]{:S(2)}) %collective-permute-start) | collective-permute-done | bytes 1048608 | tf_op jit(solution)/shard_map/ppermute | solution.py:22
  29.7 2.9 %collective-permute-start.6 = (f32[256,1024]{1,0:T(8,128)S(1)}, f32[256,1024]{1,0:T(8,128)S(1)}, u32[]{:S(2)}, u32[]{:S(2)}) collective-permute-start(f32[256,1024]{1,0:T(8,128)S(1)} %get-tuple-element.35), channel_id=1, source_target_pairs={{0,64},{32,96},{64,0},{96,32},{1,65},{33,97},{65,1},{97,33},{2,66}... | collective-permute-start | bytes 3145736 | tf_op jit(solution)/shard_map/ppermute | solution.py:22
  32.6 3.3 %early_gram.1 = (f32[4,128,256]{2,1,0:T(8,128)}, f32[4,128,256]{2,1,0:T(8,128)S(1)}, bf16[56,2,256,1024]{3,2,1,0:T(8,128)(2,1)}) custom-call(f32[256,1024]{1,0:T(8,128)S(1)} %collective-permute-done.w1, f32[256,1024]{1,0:T(8,128)S(1)} %collective-permute-done.1.w3, f32[128,256]{1,0:T(8,128)S(1)} %get-tuple-element.30.send0, ...), custom_call_target="tpu_custom_call" | custom-call | flops 1000000000 | bytes 1000 | tf_op jit(solution)/shard_map/early_gram/pallas_call | solution.py:174
  36.1 2.2 %collective-permute-done.2 = f32[4,128,256]{2,1,0:T(8,128)} collective-permute-done((f32[4,128,256]{2,1,0:T(8,128)}, f32[4,128,256]{2,1,0:T(8,128)}, u32[]{:S(2)}, u32[]{:S(2)}) %collective-permute-start.2) | collective-permute-done | bytes 524320 | tf_op jit(solution)/shard_map/ppermute | solution.py:26
  38.3 1.1 add.182
  39.4 0.8 copy-done.2
  40.2 3.1 %collective-permute-start.5 = (f32[4,32,256]{2,1,0:T(8,128)S(1)}, f32[4,32,256]{2,1,0:T(8,128)S(1)}, u32[]{:S(2)}, u32[]{:S(2)}) collective-permute-start(f32[4,32,256]{2,1,0:T(8,128)S(1)} %get-tuple-element.49), channel_id=1, source_target_pairs={{0,16},{1,5},{2,18},{3,7},{4,20},{5,1},{6,22},{7,3},{8,24},{9,13},... | collective-permute-start | bytes 393224 | tf_op jit(solution)/shard_map/ppermute | solution.py:39
  43.3 1.1 collective-permute-start.4
  44.5 0.9 collective-permute-start.3
  45.4 1.4 collective-permute-done.5
  46.8 1.5 collective-permute-done.4
  48.3 2.3 %collective-permute-done.3 = f32[4,32,256]{2,1,0:T(8,128)S(1)} collective-permute-done((f32[4,32,256]{2,1,0:T(8,128)S(1)}, f32[4,32,256]{2,1,0:T(8,128)S(1)}, u32[]{:S(2)}, u32[]{:S(2)}) %collective-permute-start.3) | collective-permute-done | bytes 131104 | tf_op jit(solution)/shard_map/ppermute | solution.py:39
  50.6 0.9 fusion.1
  51.6 3.8 %collective-permute-done.6.w2.refs_11_ = f32[256,1024]{1,0:T(8,128)S(1)} collective-permute-done((f32[256,1024]{1,0:T(8,128)S(1)}, f32[256,1024]{1,0:T(8,128)S(1)}, u32[]{:S(2)}, u32[]{:S(2)}) %collective-permute-start.6) | collective-permute-done | bytes 1048608 | tf_op jit(solution)/shard_map/ppermute | solution.py:22
  55.4 4.5 %late_gram.1 = (f32[3,128,256]{2,1,0:T(8,128)S(1)}, f32[3,128,256]{2,1,0:T(8,128)S(1)}) custom-call(f32[256,1024]{1,0:T(8,128)S(1)} %collective-permute-done.6.w2.refs_11_, bf16[56,2,256,1024]{3,2,1,0:T(8,128)(2,1)} %get-tuple-element.38.hls.refs_10_), custom_call_target="tpu_custom_call" | custom-call | flops 20000000000 | bytes 1000 | tf_op jit(solution)/shard_map/late_gram/pallas_call | solution.py:174
  60.0 1.7 %collective-permute-done.10 = f32[3,128,256]{2,1,0:T(8,128)S(1)} collective-permute-done((f32[3,128,256]{2,1,0:T(8,128)S(1)}, f32[3,128,256]{2,1,0:T(8,128)S(1)}, u32[]{:S(2)}, u32[]{:S(2)}) %collective-permute-start.10) | collective-permute-done | bytes 393248 | tf_op jit(solution)/shard_map/ppermute | solution.py:26
  61.8 3.0 %collective-permute-start.13 = (f32[3,32,256]{2,1,0:T(8,128)S(1)}, f32[3,32,256]{2,1,0:T(8,128)S(1)}, u32[]{:S(2)}, u32[]{:S(2)}) collective-permute-start(f32[3,32,256]{2,1,0:T(8,128)S(1)} %get-tuple-element.52), channel_id=1, source_target_pairs={{0,16},{1,5},{2,18},{3,7},{4,20},{5,1},{6,22},{7,3},{8,24},{9,13},... | collective-permute-start | bytes 294920 | tf_op jit(solution)/shard_map/ppermute | solution.py:39
  64.8 1.1 collective-permute-start.12
  66.0 0.9 collective-permute-start.11
  66.8 3.9 %collective-permute-start.9 = (f32[4,32,256]{2,1,0:T(8,128)S(1)}, f32[4,32,256]{2,1,0:T(8,128)S(1)}, u32[]{:S(2)}, u32[]{:S(2)}) collective-permute-start(f32[4,32,256]{2,1,0:T(8,128)S(1)} %fusion.1), channel_id=1, source_target_pairs={{0,4},{1,17},{2,6},{3,19},{4,0},{5,21},{6,2},{7,23},{8,12},{9,25},... | collective-permute-start | bytes 393224 | tf_op jit(solution)/shard_map/ppermute | solution.py:39
  70.7 0.7 collective-permute-start.8
  71.4 1.3 collective-permute-start.7
  72.8 0.4 collective-permute-done.11
  73.2 2.7 %collective-permute-start.16 = (f32[3,32,256]{2,1,0:T(8,128)S(1)}, f32[3,32,256]{2,1,0:T(8,128)S(1)}, u32[]{:S(2)}, u32[]{:S(2)}) collective-permute-start(f32[3,32,256]{2,1,0:T(8,128)S(1)} %fusion.3), channel_id=1, source_target_pairs={{0,4},{1,17},{2,6},{3,19},{4,0},{5,21},{6,2},{7,23},{8,12},{9,25},... | collective-permute-start | bytes 294920 | tf_op jit(solution)/shard_map/ppermute | solution.py:39
  75.9 1.4 collective-permute-start.15
  77.4 0.6 collective-permute-start.14
  78.0 1.4 collective-permute-done.16
  79.4 1.5 collective-permute-done.15
  80.9 2.2 %collective-permute-done.14 = f32[3,32,256]{2,1,0:T(8,128)S(1)} collective-permute-done((f32[3,32,256]{2,1,0:T(8,128)S(1)}, f32[3,32,256]{2,1,0:T(8,128)S(1)}, u32[]{:S(2)}, u32[]{:S(2)}) %collective-permute-start.14) | collective-permute-done | bytes 98336 | tf_op jit(solution)/shard_map/ppermute | solution.py:39
  83.2 1.3 collective-permute-start.19
  84.5 3.0 %collective-permute-start.18 = (f32[7,32,256]{2,1,0:T(8,128)S(1)}, f32[7,32,256]{2,1,0:T(8,128)S(1)}, u32[]{:S(2)}, u32[]{:S(2)}) collective-permute-start(f32[7,32,256]{2,1,0:T(8,128)S(1)} %pad_maximum_fusion), channel_id=1, source_target_pairs={{0,64},{32,96},{64,0},{96,32},{1,65},{33,97},{65,1},{97,33},{2,66}... | collective-permute-start | bytes 688136 | tf_op jit(solution)/shard_map/ppermute | solution.py:22
  87.6 0.9 collective-permute-start.17
  88.5 3.4 %collective-permute-done.19 = f32[7,32,256]{2,1,0:T(8,128)S(1)} collective-permute-done((f32[7,32,256]{2,1,0:T(8,128)S(1)}, f32[7,32,256]{2,1,0:T(8,128)S(1)}, u32[]{:S(2)}, u32[]{:S(2)}) %collective-permute-start.19) | collective-permute-done | bytes 229408 | tf_op jit(solution)/shard_map/ppermute | solution.py:22
  91.9 2.5 %collective-permute-done.18 = f32[7,32,256]{2,1,0:T(8,128)S(1)} collective-permute-done((f32[7,32,256]{2,1,0:T(8,128)S(1)}, f32[7,32,256]{2,1,0:T(8,128)S(1)}, u32[]{:S(2)}, u32[]{:S(2)}) %collective-permute-start.18) | collective-permute-done | bytes 229408 | tf_op jit(solution)/shard_map/ppermute | solution.py:22
  94.5 0.9 collective-permute-start.20
  95.4 1.9 %collective-permute-start.21 = (f32[10,32,256]{2,1,0:T(8,128)S(1)}, f32[10,32,256]{2,1,0:T(8,128)S(1)}, u32[]{:S(2)}, u32[]{:S(2)}) collective-permute-start(f32[10,32,256]{2,1,0:T(8,128)S(1)} %slice_dynamic-update-slice_fusion.refs_1_), channel_id=1, source_target_pairs={{0,16},{1,5},{2,18},{3,7},{4,20},{5,1},{6,22},{7,3},{8,24},{9,13},... | collective-permute-start | bytes 983048 | tf_op jit(solution)/shard_map/ppermute | solution.py:39
  97.3 1.9 %collective-permute-start.22 = (f32[10,32,256]{2,1,0:T(8,128)S(1)}, f32[10,32,256]{2,1,0:T(8,128)S(1)}, u32[]{:S(2)}, u32[]{:S(2)}) collective-permute-start(f32[10,32,256]{2,1,0:T(8,128)S(1)} %slice_dynamic-update-slice_fusion.refs_1_), channel_id=1, source_target_pairs={{0,24},{1,7},{2,26},{3,1},{4,28},{5,3},{6,30},{7,5},{8,0},{9,15},{... | collective-permute-start | bytes 983048 | tf_op jit(solution)/shard_map/ppermute | solution.py:39
  99.1 7.2 %collective-permute-done.20.refs_2_ = f32[10,32,256]{2,1,0:T(8,128)S(1)} collective-permute-done((f32[10,32,256]{2,1,0:T(8,128)S(1)}, f32[10,32,256]{2,1,0:T(8,128)S(1)}, u32[]{:S(2)}, u32[]{:S(2)}) %collective-permute-start.20) | collective-permute-done | bytes 327712 | tf_op jit(solution)/shard_map/ppermute | solution.py:39
  106.4 0.5 collective-permute-start.25
  106.9 0.4 collective-permute-done.22.refs_4_
  108.0 0.5 collective-permute-done.25.refs_7_
  108.5 0.5 collective-permute-done.26.refs_8_
  109.0 20.0 %solve.1 = (f32[1024,128]{1,0:T(8,128)}, f32[32,1024]{1,0:T(8,128)S(1)}, f32[32,1024]{1,0:T(8,128)S(1)}, f32[32,1024]{1,0:T(8,128)S(1)}, f32[32,1024]{1,0:T(8,128)S(1)}, /*index=5*/f32[72,128]{1,0:T(8,128)S(1)}) custom-call(s32[1]{0:T(128)S(6)} %copy.31.refs_0_, f32[10,32,256]{2,1,0:T(8,128)S(1)} %slice_dynamic-update-slice_fusion.refs_1_, ...), custom_call_target="tpu_custom_call" | custom-call | flops 8000000000 | bytes 9437184 | tf_op jit(solution)/shard_map/solve/pallas_call | solution.py:387
  129.2 1.1 collective-permute-done.30
  130.3 1.9 %collective-permute-start.33 = (f32[72,128]{1,0:T(8,128)S(1)}, f32[72,128]{1,0:T(8,128)S(1)}, u32[]{:S(2)}, u32[]{:S(2)}) collective-permute-start(f32[72,128]{1,0:T(8,128)S(1)} %add.225), channel_id=1, source_target_pairs={{0,16},{1,5},{2,18},{3,7},{4,20},{5,1},{6,22},{7,3},{8,24},{9,13},... | collective-permute-start | bytes 110600 | tf_op jit(solution)/shard_map/ppermute | solution.py:39
  132.1 2.0 %collective-permute-start.32 = (f32[72,128]{1,0:T(8,128)S(1)}, f32[72,128]{1,0:T(8,128)S(1)}, u32[]{:S(2)}, u32[]{:S(2)}) collective-permute-start(f32[72,128]{1,0:T(8,128)S(1)} %add.225), channel_id=1, source_target_pairs={{0,24},{1,7},{2,26},{3,1},{4,28},{5,3},{6,30},{7,5},{8,0},{9,15},{... | collective-permute-start | bytes 110600 | tf_op jit(solution)/shard_map/ppermute | solution.py:39
  134.2 1.6 collective-permute-done.33
  136.1 3.2 %collective-permute-done.31 = f32[72,128]{1,0:T(8,128)S(1)} collective-permute-done((f32[72,128]{1,0:T(8,128)S(1)}, f32[72,128]{1,0:T(8,128)S(1)}, u32[]{:S(2)}, u32[]{:S(2)}) %collective-permute-start.31) | collective-permute-done | bytes 36896 | tf_op jit(solution)/shard_map/ppermute | solution.py:39
  139.6 2.0 %collective-permute-start.35 = (f32[72,128]{1,0:T(8,128)S(1)}, f32[72,128]{1,0:T(8,128)S(1)}, u32[]{:S(2)}, u32[]{:S(2)}) collective-permute-start(f32[72,128]{1,0:T(8,128)S(1)} %add_add_fusion.3), channel_id=1, source_target_pairs={{0,6},{1,25},{2,0},{3,27},{4,2},{5,29},{6,4},{7,31},{8,14},{9,1},{... | collective-permute-start | bytes 110600 | tf_op jit(solution)/shard_map/ppermute | solution.py:39
  141.7 1.3 collective-permute-start.27
  143.1 2.4 %collective-permute-start.28 = (f32[32,1024]{1,0:T(8,128)S(1)}, f32[32,1024]{1,0:T(8,128)S(1)}, u32[]{:S(2)}, u32[]{:S(2)}) collective-permute-start(f32[32,1024]{1,0:T(8,128)S(1)} %get-tuple-element.44), channel_id=1, source_target_pairs={{0,64},{32,96},{64,0},{96,32},{1,65},{33,97},{65,1},{97,33},{2,66}... | collective-permute-start | bytes 393224 | tf_op jit(solution)/shard_map/ppermute | solution.py:22
  145.4 1.9 %collective-permute-start.29 = (f32[32,1024]{1,0:T(8,128)S(1)}, f32[32,1024]{1,0:T(8,128)S(1)}, u32[]{:S(2)}, u32[]{:S(2)}) collective-permute-start(f32[32,1024]{1,0:T(8,128)S(1)} %get-tuple-element.45), channel_id=1, source_target_pairs={{0,96},{32,0},{64,32},{96,64},{1,97},{33,1},{65,33},{97,65},{2,98}... | collective-permute-start | bytes 393224 | tf_op jit(solution)/shard_map/ppermute | solution.py:22
  147.4 0.8 collective-permute-start.37
  148.2 2.5 %collective-permute-start.38 = (f32[72,128]{1,0:T(8,128)S(1)}, f32[72,128]{1,0:T(8,128)S(1)}, u32[]{:S(2)}, u32[]{:S(2)}) collective-permute-start(f32[72,128]{1,0:T(8,128)S(1)} %add_add_fusion.2.refs_0_), channel_id=1, source_target_pairs={{0,96},{32,0},{64,32},{96,64},{1,97},{33,1},{65,33},{97,65},{2,98}... | collective-permute-start | bytes 110600 | tf_op jit(solution)/shard_map/ppermute | solution.py:22
  150.7 0.4 collective-permute-start.39
  151.1 0.8 join_columns.1
  151.9 0.6 collective-permute-done.37.refs_1_
  152.6 3.5 %collective-permute-done.39.refs_3_ = f32[72,128]{1,0:T(8,128)S(1)} collective-permute-done((f32[72,128]{1,0:T(8,128)S(1)}, f32[72,128]{1,0:T(8,128)S(1)}, u32[]{:S(2)}, u32[]{:S(2)}) %collective-permute-start.39) | collective-permute-done | bytes 36896 | tf_op jit(solution)/shard_map/ppermute | solution.py:22
  156.1 0.8 unpack_sum.1
  (51 shorter events, 1.7 us)
Async XLA Ops:
  0.6 108.3 %copy-start.1 = (f32[1024,128]{1,0:T(8,128)S(1)}, f32[1024,128]{1,0:T(8,128)}, u32[]{:S(2)}) copy-start(f32[1024,128]{1,0:T(8,128)} %refs_9_.1) | copy-start | bytes 1572868
  3.1 26.5 %collective-permute-start = (f32[256,1024]{1,0:T(8,128)}, f32[256,1024]{1,0:T(8,128)S(1)}, u32[]{:S(2)}, u32[]{:S(2)}) collective-permute-start(f32[256,1024]{1,0:T(8,128)} %get-tuple-element.25), channel_id=1, source_target_pairs={{0,32},{32,64},{64,96},{96,0},{1,33},{33,65},{65,97},{97,1},{2,34}... | collective-permute-start | bytes 3145736 | tf_op jit(solution)/shard_map/ppermute | solution.py:22
  4.9 24.8 %collective-permute-start.1 = (f32[256,1024]{1,0:T(8,128)}, f32[256,1024]{1,0:T(8,128)S(1)}, u32[]{:S(2)}, u32[]{:S(2)}) collective-permute-start(f32[256,1024]{1,0:T(8,128)} %get-tuple-element.26), channel_id=1, source_target_pairs={{0,96},{32,0},{64,32},{96,64},{1,97},{33,1},{65,33},{97,65},{2,98}... | collective-permute-start | bytes 3145736 | tf_op jit(solution)/shard_map/ppermute | solution.py:22
  6.4 2.2 %copy-start = (f32[256,4096]{1,0:T(8,128)S(1)}, f32[256,4096]{1,0:T(8,128)}, u32[]{:S(2)}) copy-start(f32[256,4096]{1,0:T(8,128)} %slab.3) | copy-start | bytes 12582916
  29.7 25.7 %collective-permute-start.6 = (f32[256,1024]{1,0:T(8,128)S(1)}, f32[256,1024]{1,0:T(8,128)S(1)}, u32[]{:S(2)}, u32[]{:S(2)}) collective-permute-start(f32[256,1024]{1,0:T(8,128)S(1)} %get-tuple-element.35), channel_id=1, source_target_pairs={{0,64},{32,96},{64,0},{96,32},{1,65},{33,97},{65,1},{97,33},{2,66}... | collective-permute-start | bytes 3145736 | tf_op jit(solution)/shard_map/ppermute | solution.py:22
  35.9 2.3 %collective-permute-start.2 = (f32[4,128,256]{2,1,0:T(8,128)}, f32[4,128,256]{2,1,0:T(8,128)}, u32[]{:S(2)}, u32[]{:S(2)}) collective-permute-start(f32[4,128,256]{2,1,0:T(8,128)} %get-tuple-element.34), channel_id=1, source_target_pairs={{0,1},{1,0},{2,3},{3,2},{4,5},{5,4},{6,7},{7,6},{8,9},{9,8},{10,11... | collective-permute-start | bytes 1572872 | tf_op jit(solution)/shard_map/ppermute | solution.py:26
  39.4 0.8 copy-start.2
  40.2 6.6 %collective-permute-start.5 = (f32[4,32,256]{2,1,0:T(8,128)S(1)}, f32[4,32,256]{2,1,0:T(8,128)S(1)}, u32[]{:S(2)}, u32[]{:S(2)}) collective-permute-start(f32[4,32,256]{2,1,0:T(8,128)S(1)} %get-tuple-element.49), channel_id=1, source_target_pairs={{0,16},{1,5},{2,18},{3,7},{4,20},{5,1},{6,22},{7,3},{8,24},{9,13},... | collective-permute-start | bytes 393224 | tf_op jit(solution)/shard_map/ppermute | solution.py:39
  43.3 5.0 %collective-permute-start.4 = (f32[4,32,256]{2,1,0:T(8,128)S(1)}, f32[4,32,256]{2,1,0:T(8,128)S(1)}, u32[]{:S(2)}, u32[]{:S(2)}) collective-permute-start(f32[4,32,256]{2,1,0:T(8,128)S(1)} %get-tuple-element.48), channel_id=1, source_target_pairs={{0,24},{1,7},{2,26},{3,1},{4,28},{5,3},{6,30},{7,5},{8,0},{9,15},{... | collective-permute-start | bytes 393224 | tf_op jit(solution)/shard_map/ppermute | solution.py:39
  44.5 6.2 %collective-permute-start.3 = (f32[4,32,256]{2,1,0:T(8,128)S(1)}, f32[4,32,256]{2,1,0:T(8,128)S(1)}, u32[]{:S(2)}, u32[]{:S(2)}) collective-permute-start(f32[4,32,256]{2,1,0:T(8,128)S(1)} %get-tuple-element.47), channel_id=1, source_target_pairs={{0,8},{1,3},{2,10},{3,5},{4,12},{5,7},{6,14},{7,1},{8,16},{9,11},{... | collective-permute-start | bytes 393224 | tf_op jit(solution)/shard_map/ppermute | solution.py:39
  59.9 1.8 %collective-permute-start.10 = (f32[3,128,256]{2,1,0:T(8,128)S(1)}, f32[3,128,256]{2,1,0:T(8,128)S(1)}, u32[]{:S(2)}, u32[]{:S(2)}) collective-permute-start(f32[3,128,256]{2,1,0:T(8,128)S(1)} %get-tuple-element.40), channel_id=1, source_target_pairs={{0,1},{1,0},{2,3},{3,2},{4,5},{5,4},{6,7},{7,6},{8,9},{9,8},{10,11... | collective-permute-start | bytes 1179656 | tf_op jit(solution)/shard_map/ppermute | solution.py:26
  61.8 9.6 %collective-permute-start.13 = (f32[3,32,256]{2,1,0:T(8,128)S(1)}, f32[3,32,256]{2,1,0:T(8,128)S(1)}, u32[]{:S(2)}, u32[]{:S(2)}) collective-permute-start(f32[3,32,256]{2,1,0:T(8,128)S(1)} %get-tuple-element.52), channel_id=1, source_target_pairs={{0,16},{1,5},{2,18},{3,7},{4,20},{5,1},{6,22},{7,3},{8,24},{9,13},... | collective-permute-start | bytes 294920 | tf_op jit(solution)/shard_map/ppermute | solution.py:39
  64.8 7.9 %collective-permute-start.12 = (f32[3,32,256]{2,1,0:T(8,128)S(1)}, f32[3,32,256]{2,1,0:T(8,128)S(1)}, u32[]{:S(2)}, u32[]{:S(2)}) collective-permute-start(f32[3,32,256]{2,1,0:T(8,128)S(1)} %get-tuple-element.51), channel_id=1, source_target_pairs={{0,24},{1,7},{2,26},{3,1},{4,28},{5,3},{6,30},{7,5},{8,0},{9,15},{... | collective-permute-start | bytes 294920 | tf_op jit(solution)/shard_map/ppermute | solution.py:39
  66.0 7.2 %collective-permute-start.11 = (f32[3,32,256]{2,1,0:T(8,128)S(1)}, f32[3,32,256]{2,1,0:T(8,128)S(1)}, u32[]{:S(2)}, u32[]{:S(2)}) collective-permute-start(f32[3,32,256]{2,1,0:T(8,128)S(1)} %get-tuple-element.50), channel_id=1, source_target_pairs={{0,8},{1,3},{2,10},{3,5},{4,12},{5,7},{6,14},{7,1},{8,16},{9,11},{... | collective-permute-start | bytes 294920 | tf_op jit(solution)/shard_map/ppermute | solution.py:39
  66.8 10.5 %collective-permute-start.9 = (f32[4,32,256]{2,1,0:T(8,128)S(1)}, f32[4,32,256]{2,1,0:T(8,128)S(1)}, u32[]{:S(2)}, u32[]{:S(2)}) collective-permute-start(f32[4,32,256]{2,1,0:T(8,128)S(1)} %fusion.1), channel_id=1, source_target_pairs={{0,4},{1,17},{2,6},{3,19},{4,0},{5,21},{6,2},{7,23},{8,12},{9,25},... | collective-permute-start | bytes 393224 | tf_op jit(solution)/shard_map/ppermute | solution.py:39
  70.7 7.2 %collective-permute-start.8 = (f32[4,32,256]{2,1,0:T(8,128)S(1)}, f32[4,32,256]{2,1,0:T(8,128)S(1)}, u32[]{:S(2)}, u32[]{:S(2)}) collective-permute-start(f32[4,32,256]{2,1,0:T(8,128)S(1)} %fusion.1), channel_id=1, source_target_pairs={{0,6},{1,25},{2,0},{3,27},{4,2},{5,29},{6,4},{7,31},{8,14},{9,1},{... | collective-permute-start | bytes 393224 | tf_op jit(solution)/shard_map/ppermute | solution.py:39
  71.4 6.5 %collective-permute-start.7 = (f32[4,32,256]{2,1,0:T(8,128)S(1)}, f32[4,32,256]{2,1,0:T(8,128)S(1)}, u32[]{:S(2)}, u32[]{:S(2)}) collective-permute-start(f32[4,32,256]{2,1,0:T(8,128)S(1)} %fusion.1), channel_id=1, source_target_pairs={{0,2},{1,9},{2,4},{3,11},{4,6},{5,13},{6,0},{7,15},{8,10},{9,17},{... | collective-permute-start | bytes 393224 | tf_op jit(solution)/shard_map/ppermute | solution.py:39
  73.2 6.2 %collective-permute-start.16 = (f32[3,32,256]{2,1,0:T(8,128)S(1)}, f32[3,32,256]{2,1,0:T(8,128)S(1)}, u32[]{:S(2)}, u32[]{:S(2)}) collective-permute-start(f32[3,32,256]{2,1,0:T(8,128)S(1)} %fusion.3), channel_id=1, source_target_pairs={{0,4},{1,17},{2,6},{3,19},{4,0},{5,21},{6,2},{7,23},{8,12},{9,25},... | collective-permute-start | bytes 294920 | tf_op jit(solution)/shard_map/ppermute | solution.py:39
  75.9 5.0 %collective-permute-start.15 = (f32[3,32,256]{2,1,0:T(8,128)S(1)}, f32[3,32,256]{2,1,0:T(8,128)S(1)}, u32[]{:S(2)}, u32[]{:S(2)}) collective-permute-start(f32[3,32,256]{2,1,0:T(8,128)S(1)} %fusion.3), channel_id=1, source_target_pairs={{0,6},{1,25},{2,0},{3,27},{4,2},{5,29},{6,4},{7,31},{8,14},{9,1},{... | collective-permute-start | bytes 294920 | tf_op jit(solution)/shard_map/ppermute | solution.py:39
  77.4 5.8 %collective-permute-start.14 = (f32[3,32,256]{2,1,0:T(8,128)S(1)}, f32[3,32,256]{2,1,0:T(8,128)S(1)}, u32[]{:S(2)}, u32[]{:S(2)}) collective-permute-start(f32[3,32,256]{2,1,0:T(8,128)S(1)} %fusion.3), channel_id=1, source_target_pairs={{0,2},{1,9},{2,4},{3,11},{4,6},{5,13},{6,0},{7,15},{8,10},{9,17},{... | collective-permute-start | bytes 294920 | tf_op jit(solution)/shard_map/ppermute | solution.py:39
  83.2 8.7 %collective-permute-start.19 = (f32[7,32,256]{2,1,0:T(8,128)S(1)}, f32[7,32,256]{2,1,0:T(8,128)S(1)}, u32[]{:S(2)}, u32[]{:S(2)}) collective-permute-start(f32[7,32,256]{2,1,0:T(8,128)S(1)} %pad_maximum_fusion), channel_id=1, source_target_pairs={{0,32},{32,64},{64,96},{96,0},{1,33},{33,65},{65,97},{97,1},{2,34}... | collective-permute-start | bytes 688136 | tf_op jit(solution)/shard_map/ppermute | solution.py:22
  84.5 9.8 %collective-permute-start.18 = (f32[7,32,256]{2,1,0:T(8,128)S(1)}, f32[7,32,256]{2,1,0:T(8,128)S(1)}, u32[]{:S(2)}, u32[]{:S(2)}) collective-permute-start(f32[7,32,256]{2,1,0:T(8,128)S(1)} %pad_maximum_fusion), channel_id=1, source_target_pairs={{0,64},{32,96},{64,0},{96,32},{1,65},{33,97},{65,1},{97,33},{2,66}... | collective-permute-start | bytes 688136 | tf_op jit(solution)/shard_map/ppermute | solution.py:22
  87.6 6.8 %collective-permute-start.17 = (f32[7,32,256]{2,1,0:T(8,128)S(1)}, f32[7,32,256]{2,1,0:T(8,128)S(1)}, u32[]{:S(2)}, u32[]{:S(2)}) collective-permute-start(f32[7,32,256]{2,1,0:T(8,128)S(1)} %pad_maximum_fusion), channel_id=1, source_target_pairs={{0,96},{32,0},{64,32},{96,64},{1,97},{33,1},{65,33},{97,65},{2,98}... | collective-permute-start | bytes 688136 | tf_op jit(solution)/shard_map/ppermute | solution.py:22
  94.5 11.9 %collective-permute-start.20 = (f32[10,32,256]{2,1,0:T(8,128)S(1)}, f32[10,32,256]{2,1,0:T(8,128)S(1)}, u32[]{:S(2)}, u32[]{:S(2)}) collective-permute-start(f32[10,32,256]{2,1,0:T(8,128)S(1)} %slice_dynamic-update-slice_fusion.refs_1_), channel_id=1, source_target_pairs={{0,8},{1,3},{2,10},{3,5},{4,12},{5,7},{6,14},{7,1},{8,16},{9,11},{... | collective-permute-start | bytes 983048 | tf_op jit(solution)/shard_map/ppermute | solution.py:39
  95.4 11.0 %collective-permute-start.21 = (f32[10,32,256]{2,1,0:T(8,128)S(1)}, f32[10,32,256]{2,1,0:T(8,128)S(1)}, u32[]{:S(2)}, u32[]{:S(2)}) collective-permute-start(f32[10,32,256]{2,1,0:T(8,128)S(1)} %slice_dynamic-update-slice_fusion.refs_1_), channel_id=1, source_target_pairs={{0,16},{1,5},{2,18},{3,7},{4,20},{5,1},{6,22},{7,3},{8,24},{9,13},... | collective-permute-start | bytes 983048 | tf_op jit(solution)/shard_map/ppermute | solution.py:39
  97.3 10.0 %collective-permute-start.22 = (f32[10,32,256]{2,1,0:T(8,128)S(1)}, f32[10,32,256]{2,1,0:T(8,128)S(1)}, u32[]{:S(2)}, u32[]{:S(2)}) collective-permute-start(f32[10,32,256]{2,1,0:T(8,128)S(1)} %slice_dynamic-update-slice_fusion.refs_1_), channel_id=1, source_target_pairs={{0,24},{1,7},{2,26},{3,1},{4,28},{5,3},{6,30},{7,5},{8,0},{9,15},{... | collective-permute-start | bytes 983048 | tf_op jit(solution)/shard_map/ppermute | solution.py:39
  99.1 8.8 %collective-permute-start.23 = (f32[10,32,256]{2,1,0:T(8,128)S(1)}, f32[10,32,256]{2,1,0:T(8,128)S(1)}, u32[]{:S(2)}, u32[]{:S(2)}) collective-permute-start(f32[10,32,256]{2,1,0:T(8,128)S(1)} %slice_dynamic-update-slice_fusion.refs_1_), channel_id=1, source_target_pairs={{0,1},{1,0},{2,3},{3,2},{4,5},{5,4},{6,7},{7,6},{8,9},{9,8},{10,11... | collective-permute-start | bytes 983048 | tf_op jit(solution)/shard_map/ppermute | solution.py:26
  106.4 1.6 %collective-permute-start.24 = (f32[10,32,256]{2,1,0:T(8,128)S(1)}, f32[10,32,256]{2,1,0:T(8,128)S(1)}, u32[]{:S(2)}, u32[]{:S(2)}) collective-permute-start(f32[10,32,256]{2,1,0:T(8,128)S(1)} %collective-permute-done.20.refs_2_), channel_id=1, source_target_pairs={{0,1},{1,0},{2,3},{3,2},{4,5},{5,4},{6,7},{7,6},{8,9},{9,8},{10,11... | collective-permute-start | bytes 983048 | tf_op jit(solution)/shard_map/ppermute | solution.py:26
  106.4 2.1 %collective-permute-start.25 = (f32[10,32,256]{2,1,0:T(8,128)S(1)}, f32[10,32,256]{2,1,0:T(8,128)S(1)}, u32[]{:S(2)}, u32[]{:S(2)}) collective-permute-start(f32[10,32,256]{2,1,0:T(8,128)S(1)} %collective-permute-done.21.refs_3_), channel_id=1, source_target_pairs={{0,1},{1,0},{2,3},{3,2},{4,5},{5,4},{6,7},{7,6},{8,9},{9,8},{10,11... | collective-permute-start | bytes 983048 | tf_op jit(solution)/shard_map/ppermute | solution.py:26
  107.3 1.7 %collective-permute-start.26 = (f32[10,32,256]{2,1,0:T(8,128)S(1)}, f32[10,32,256]{2,1,0:T(8,128)S(1)}, u32[]{:S(2)}, u32[]{:S(2)}) collective-permute-start(f32[10,32,256]{2,1,0:T(8,128)S(1)} %collective-permute-done.22.refs_4_), channel_id=1, source_target_pairs={{0,1},{1,0},{2,3},{3,2},{4,5},{5,4},{6,7},{7,6},{8,9},{9,8},{10,11... | collective-permute-start | bytes 983048 | tf_op jit(solution)/shard_map/ppermute | solution.py:26
  129.0 1.3 collective-permute-start.30
  130.3 5.5 %collective-permute-start.33 = (f32[72,128]{1,0:T(8,128)S(1)}, f32[72,128]{1,0:T(8,128)S(1)}, u32[]{:S(2)}, u32[]{:S(2)}) collective-permute-start(f32[72,128]{1,0:T(8,128)S(1)} %add.225), channel_id=1, source_target_pairs={{0,16},{1,5},{2,18},{3,7},{4,20},{5,1},{6,22},{7,3},{8,24},{9,13},... | collective-permute-start | bytes 110600 | tf_op jit(solution)/shard_map/ppermute | solution.py:39
  132.1 4.0 %collective-permute-start.32 = (f32[72,128]{1,0:T(8,128)S(1)}, f32[72,128]{1,0:T(8,128)S(1)}, u32[]{:S(2)}, u32[]{:S(2)}) collective-permute-start(f32[72,128]{1,0:T(8,128)S(1)} %add.225), channel_id=1, source_target_pairs={{0,24},{1,7},{2,26},{3,1},{4,28},{5,3},{6,30},{7,5},{8,0},{9,15},{... | collective-permute-start | bytes 110600 | tf_op jit(solution)/shard_map/ppermute | solution.py:39
  134.1 5.2 %collective-permute-start.31 = (f32[72,128]{1,0:T(8,128)S(1)}, f32[72,128]{1,0:T(8,128)S(1)}, u32[]{:S(2)}, u32[]{:S(2)}) collective-permute-start(f32[72,128]{1,0:T(8,128)S(1)} %add.225), channel_id=1, source_target_pairs={{0,8},{1,3},{2,10},{3,5},{4,12},{5,7},{6,14},{7,1},{8,16},{9,11},{... | collective-permute-start | bytes 110600 | tf_op jit(solution)/shard_map/ppermute | solution.py:39
  139.3 6.1 %collective-permute-start.36 = (f32[72,128]{1,0:T(8,128)S(1)}, f32[72,128]{1,0:T(8,128)S(1)}, u32[]{:S(2)}, u32[]{:S(2)}) collective-permute-start(f32[72,128]{1,0:T(8,128)S(1)} %add_add_fusion.3), channel_id=1, source_target_pairs={{0,4},{1,17},{2,6},{3,19},{4,0},{5,21},{6,2},{7,23},{8,12},{9,25},... | collective-permute-start | bytes 110600 | tf_op jit(solution)/shard_map/ppermute | solution.py:39
  139.6 7.7 %collective-permute-start.35 = (f32[72,128]{1,0:T(8,128)S(1)}, f32[72,128]{1,0:T(8,128)S(1)}, u32[]{:S(2)}, u32[]{:S(2)}) collective-permute-start(f32[72,128]{1,0:T(8,128)S(1)} %add_add_fusion.3), channel_id=1, source_target_pairs={{0,6},{1,25},{2,0},{3,27},{4,2},{5,29},{6,4},{7,31},{8,14},{9,1},{... | collective-permute-start | bytes 110600 | tf_op jit(solution)/shard_map/ppermute | solution.py:39
  141.6 5.7 %collective-permute-start.34 = (f32[72,128]{1,0:T(8,128)S(1)}, f32[72,128]{1,0:T(8,128)S(1)}, u32[]{:S(2)}, u32[]{:S(2)}) collective-permute-start(f32[72,128]{1,0:T(8,128)S(1)} %add_add_fusion.3), channel_id=1, source_target_pairs={{0,2},{1,9},{2,4},{3,11},{4,6},{5,13},{6,0},{7,15},{8,10},{9,17},{... | collective-permute-start | bytes 110600 | tf_op jit(solution)/shard_map/ppermute | solution.py:39
  141.7 8.9 %collective-permute-start.27 = (f32[32,1024]{1,0:T(8,128)S(1)}, f32[32,1024]{1,0:T(8,128)S(1)}, u32[]{:S(2)}, u32[]{:S(2)}) collective-permute-start(f32[32,1024]{1,0:T(8,128)S(1)} %get-tuple-element.43), channel_id=1, source_target_pairs={{0,32},{32,64},{64,96},{96,0},{1,33},{33,65},{65,97},{97,1},{2,34}... | collective-permute-start | bytes 393224 | tf_op jit(solution)/shard_map/ppermute | solution.py:22
  143.1 8.0 %collective-permute-start.28 = (f32[32,1024]{1,0:T(8,128)S(1)}, f32[32,1024]{1,0:T(8,128)S(1)}, u32[]{:S(2)}, u32[]{:S(2)}) collective-permute-start(f32[32,1024]{1,0:T(8,128)S(1)} %get-tuple-element.44), channel_id=1, source_target_pairs={{0,64},{32,96},{64,0},{96,32},{1,65},{33,97},{65,1},{97,33},{2,66}... | collective-permute-start | bytes 393224 | tf_op jit(solution)/shard_map/ppermute | solution.py:22
  145.4 5.7 %collective-permute-start.29 = (f32[32,1024]{1,0:T(8,128)S(1)}, f32[32,1024]{1,0:T(8,128)S(1)}, u32[]{:S(2)}, u32[]{:S(2)}) collective-permute-start(f32[32,1024]{1,0:T(8,128)S(1)} %get-tuple-element.45), channel_id=1, source_target_pairs={{0,96},{32,0},{64,32},{96,64},{1,97},{33,1},{65,33},{97,65},{2,98}... | collective-permute-start | bytes 393224 | tf_op jit(solution)/shard_map/ppermute | solution.py:22
  147.4 5.2 %collective-permute-start.37 = (f32[72,128]{1,0:T(8,128)S(1)}, f32[72,128]{1,0:T(8,128)S(1)}, u32[]{:S(2)}, u32[]{:S(2)}) collective-permute-start(f32[72,128]{1,0:T(8,128)S(1)} %add_add_fusion.2.refs_0_), channel_id=1, source_target_pairs={{0,32},{32,64},{64,96},{96,0},{1,33},{33,65},{65,97},{97,1},{2,34}... | collective-permute-start | bytes 110600 | tf_op jit(solution)/shard_map/ppermute | solution.py:22
  148.2 4.4 %collective-permute-start.38 = (f32[72,128]{1,0:T(8,128)S(1)}, f32[72,128]{1,0:T(8,128)S(1)}, u32[]{:S(2)}, u32[]{:S(2)}) collective-permute-start(f32[72,128]{1,0:T(8,128)S(1)} %add_add_fusion.2.refs_0_), channel_id=1, source_target_pairs={{0,96},{32,0},{64,32},{96,64},{1,97},{33,1},{65,33},{97,65},{2,98}... | collective-permute-start | bytes 110600 | tf_op jit(solution)/shard_map/ppermute | solution.py:22
  150.7 5.5 %collective-permute-start.39 = (f32[72,128]{1,0:T(8,128)S(1)}, f32[72,128]{1,0:T(8,128)S(1)}, u32[]{:S(2)}, u32[]{:S(2)}) collective-permute-start(f32[72,128]{1,0:T(8,128)S(1)} %add_add_fusion.2.refs_0_), channel_id=1, source_target_pairs={{0,64},{32,96},{64,0},{96,32},{1,65},{33,97},{65,1},{97,33},{2,66}... | collective-permute-start | bytes 110600 | tf_op jit(solution)/shard_map/ppermute | solution.py:22
